TPU v7x, 32 devices: a whole 2x2x4 slice. The times are simulated.
32 devices in a mesh: parts: 2 (over y), col: 4 (over z), row: 4 (over x, core).
Axes of the slice: x: 2, y: 2, z: 4, core: 2. Of those that a mesh axis runs over, the one named last changes fastest.
Arguments:
- grad_table: bfloat16 [16384, 32768], P(('parts', 'row'), 'col'), parts along dimension 0, may hold values from -60 to 60
- prev_embed: bfloat16 [8192, 512], P('row', 'col'), may hold values from -6 to 6
- next_embed: bfloat16 [32768, 512], P('col', 'row'), may hold values from -6 to 6
- log_norm: float32 [16384], P(('parts', 'row')), parts along dimension 0, may hold values from 9 to 11
Outputs:
- prev_grad: float32 [16384, 512], P(('parts', 'row'), 'col'), parts along dimension 0
- next_grad: float32 [65536, 512], P(('parts', 'col'), 'row'), parts along dimension 0
There are 2 independent parts, one for each index of `parts`. A program takes and returns all parts, laid end to end along the dimension named above; an argument that names none is the same for every part. Nothing has to cross between parts.
All inputs are finite; a program needn't handle non-finite values.
Results may differ from a plain program's by a relative error of at most 0.0025.
Values may be sent and summed in bfloat16 or wider, within the bound.
A program may use at most 256 MiB of HBM per device.

v0:
```python
import math

import jax
import jax.numpy as jnp
from jax import lax
from jax.sharding import PartitionSpec as P

E = 512


def body(grad_table, prev_embed, next_embed, log_norm):
    scale = 2.0 / math.sqrt(E)
    prev_full = lax.all_gather(prev_embed, "col", axis=1, tiled=True)
    next_full = lax.all_gather(next_embed, "row", axis=1, tiled=True)
    logits = lax.dot_general(
        prev_full, next_full, (((1,), (1,)), ((), ())), preferred_element_type=jnp.float32
    )
    probs = jnp.exp(scale * logits - log_norm[:, None])
    widened = grad_table.astype(jnp.float32)
    row_dot = lax.psum(jnp.sum(widened * probs, axis=1), "col")
    dlogits = (scale * probs * (widened - row_dot[:, None])).astype(jnp.bfloat16)
    next_terms = lax.dot_general(
        dlogits, prev_full, (((0,), (0,)), ((), ())), preferred_element_type=jnp.float32
    )
    next_grad = lax.psum_scatter(next_terms, "row", scatter_dimension=1, tiled=True)
    prev_terms = jnp.dot(dlogits, next_full, preferred_element_type=jnp.float32)
    prev_grad = lax.psum_scatter(prev_terms, "col", scatter_dimension=1, tiled=True)
    return (prev_grad, next_grad)


def solution(mesh):
    placed = (P(("parts", "row"), "col"), P("row", "col"), P("col", "row"), P(("parts", "row")))
    return jax.shard_map(
        body,
        mesh=mesh,
        in_specs=placed,
        out_specs=(P(("parts", "row"), "col"), P(("parts", "col"), "row")),
        check_vma=False,
    )
```

profile of v0, /device:TPU:9, one launch (start us, length us, event | category | flops | bytes accessed | tf_op | source)
XLA Modules:
  0.0 449.1 jit_solution(12746472674789742065)
XLA Ops:
  7.2 0.0 all-gather.3.cloned.1.call-start
  7.2 0.7 all-gather.3.cloned.1.call-update
  7.9 0.0 all-gather.5.cloned.1.call-start
  7.9 0.7 all-gather.5.cloned.1.call-update
  8.6 0.0 copy-start
  8.7 0.0 reduce-scatter.3.cloned.1.call-start
  8.7 46.8 %all-gather.3.cloned.1.call-done = bf16[2048,512]{1,0:T(8,128)(2,1)} async-done(((bf16[2048,128]{1,0:T(8,128)(2,1)}), bf16[2048,512]{1,0:T(8,128)(2,1)}) %all-gather.3.cloned.1.call-update) | async-done | bytes 2097168 | tf_op jit(solution)/shard_map/all_gather | solution.py:13
  55.5 61.1 %all-gather.5.cloned.1.call-done = bf16[8192,512]{1,0:T(8,128)(2,1)} async-done(((bf16[8192,128]{1,0:T(8,128)(2,1)}), bf16[8192,512]{1,0:T(8,128)(2,1)}) %all-gather.5.cloned.1.call-update) | async-done | bytes 8388624 | tf_op jit(solution)/shard_map/all_gather | solution.py:14
  116.6 42.8 %fusion = (f32[2048]{0:T(1024)S(1)}, f32[2048,8192]{1,0:T(8,128)}) fusion(bf16[2048,8192]{1,0:T(8,128)(2,1)} %param.4, f32[2048]{0:T(1024)} %param.7, bf16[2048,512]{1,0:T(8,128)(2,1)} %all-gather.3.cloned.1.call-done, bf16[8192,512]{1,0:T(8,128)(2,1)} %all-gather.5.cloned.1.call-done), kind=kOutput, calls=%fused_computation.2 | convolution fusion | flops 17263753216 | bytes 111165440 | tf_op jit(solution)/shard_map/dot_general | solution.py:15
  159.4 7.0 %psum.7 = f32[2048]{0:T(1024)S(1)} all-reduce(f32[2048]{0:T(1024)S(1)} %get-tuple-element.2), channel_id=1, replica_groups=mesh['parts'=2,'col'=4,'row'=4] {'col'}, use_global_device_ids=true, to_apply=%region_1.0 | all-reduce | flops 2048 | bytes 16384 | tf_op jit(solution)/shard_map/psum | solution.py:20
  166.4 0.0 copy-done
  166.4 42.8 %fusion.2 = bf16[2048,8192]{1,0:T(8,128)(2,1)} fusion(bf16[2048,8192]{1,0:T(8,128)(2,1)} %param.4, f32[2048,8192]{1,0:T(8,128)} %get-tuple-element.3, f32[2048]{0:T(1024)S(1)} %psum.7, f32[2048]{0:T(1024)S(1)} %copy-done), kind=kLoop, calls=%fused_computation.4 | loop fusion | flops 117440512 | bytes 134234112 | tf_op jit(solution)/shard_map/convert_element_type | solution.py:21
  209.2 0.0 copy-start.1
  209.2 24.9 %fusion.3 = f32[2048,512]{1,0:T(8,128)} fusion(bf16[2048,8192]{1,0:T(8,128)(2,1)} %fusion.2, bf16[8192,512]{1,0:T(8,128)(2,1)} %all-gather.5.cloned.1.call-done), kind=kOutput, calls=%fused_computation.6 | convolution fusion | flops 17179869184 | bytes 46137344 | tf_op jit(solution)/shard_map/dot_general | solution.py:26
  234.1 0.0 reduce-scatter.3.cloned.1.call-update
  234.1 0.2 reduce-scatter.5.cloned.1.call-start
  234.3 0.0 copy-done.1
  234.4 26.9 %fusion.4 = f32[8192,512]{1,0:T(8,128)} fusion(bf16[2048,8192]{1,0:T(8,128)(2,1)} %fusion.2, bf16[2048,512]{1,0:T(8,128)(2,1)S(1)} %copy-done.1), kind=kOutput, calls=%fused_computation.7 | convolution fusion | flops 17179869184 | bytes 52428800 | tf_op jit(solution)/shard_map/dot_general | solution.py:22
  261.2 0.0 reduce-scatter.5.cloned.1.call-update
  261.3 51.5 %reduce-scatter.3.cloned.1.call-done = f32[2048,128]{1,0:T(8,128)} async-done(((f32[2048,512]{1,0:T(8,128)}), f32[2048,128]{1,0:T(8,128)}) %reduce-scatter.3.cloned.1.call-update) | async-done | bytes 1048592 | tf_op jit(solution)/shard_map/reduce_scatter | solution.py:27
  312.8 129.8 %reduce-scatter.5.cloned.1.call-done = f32[8192,128]{1,0:T(8,128)} async-done(((f32[8192,512]{1,0:T(8,128)}), f32[8192,128]{1,0:T(8,128)}) %reduce-scatter.5.cloned.1.call-update) | async-done | bytes 4194320 | tf_op jit(solution)/shard_map/reduce_scatter | solution.py:25
Async XLA Ops:
  7.2 48.4 %all-gather.3.cloned.1.call-start = ((), (), s32[]{:S(2)}) async-start(), calls=%async_computation.2 | async-start | bytes 2621440 | tf_op jit(solution)/shard_map/all_gather | solution.py:13
  7.9 108.7 %all-gather.5.cloned.1.call-start = ((), (), s32[]{:S(2)}) async-start(), calls=%async_computation.3 | async-start | bytes 10485760 | tf_op jit(solution)/shard_map/all_gather | solution.py:14
  8.6 157.7 %copy-start = (f32[2048]{0:T(1024)S(1)}, f32[2048]{0:T(1024)}, u32[]{:S(2)}) copy-start(f32[2048]{0:T(1024)} %param.7) | copy-start | bytes 24580
  8.7 304.1 %reduce-scatter.3.cloned.1.call-start = ((), (), s32[]{:S(2)}) async-start(), calls=%async_computation.4 | async-start | bytes 5242880 | tf_op jit(solution)/shard_map/reduce_scatter | solution.py:27
  209.2 25.1 %copy-start.1 = (bf16[2048,512]{1,0:T(8,128)(2,1)S(1)}, bf16[2048,512]{1,0:T(8,128)(2,1)}, u32[]{:S(2)}) copy-start(bf16[2048,512]{1,0:T(8,128)(2,1)} %all-gather.3.cloned.1.call-done) | copy-start | bytes 6291460
  234.1 208.4 %reduce-scatter.5.cloned.1.call-start = ((), (), s32[]{:S(2)}) async-start(), calls=%async_computation.5 | async-start | bytes 20971520 | tf_op jit(solution)/shard_map/reduce_scatter | solution.py:25
Sparse Core Ops, SparseCore 0:
  9.6 45.9 all-gather.2
  57.1 59.5 all-gather.4
  234.2 78.4 reduce-scatter.2
  316.0 126.5 reduce-scatter.4
where the time goes:
time: 451 us; the launch traced here: 449 us
  waiting for transfers between devices  291 us (65%)
  matrix products  94.5 us (21%)
  other arithmetic  42.8 us (9%)
  between operations  13.8 us (3%)
  blocking collectives  6.97 us (2%)
    reduce_scatter x1, waiting for transfers between devices, body(): lax.psum_scatter(next_terms, 'row', scatter_dimension=1, tiled=True)  130 us
    all_gather x1, waiting for transfers between devices, body(): next_full = lax.all_gather(next_embed, 'row', axis=1, tiled=True)  61.1 us
    reduce_scatter x1, waiting for transfers between devices, body(): lax.psum_scatter(prev_terms, 'col', scatter_dimension=1, tiled=True)  51.5 us
    all_gather x1, waiting for transfers between devices, body(): prev_full = lax.all_gather(prev_embed, 'col', axis=1, tiled=True)  46.8 us
    convert_element_type x1, other arithmetic, body(): (scale * probs * (widened - row_dot[:, None])).astype(jnp.bfloat16)  42.8 us
    dot_general x1, matrix products, body(): lax.dot_general(prev_full, next_full, (((1,), (1,)), ((), ())), preferred...  42.8 us
    dot_general x1, matrix products, body(): lax.dot_general(dlogits, prev_full, (((0,), (0,)), ((), ())), preferred_e...  26.9 us
    dot_general x1, matrix products, body(): prev_terms = jnp.dot(dlogits, next_full, preferred_element_type=jnp.float32)  24.9 us
  transfers between devices with their start and end apart: 4, of which 4 were waited for; matrix products, arithmetic and copies ran while one was open for 6% of the time, Pallas kernels for 0%

commit v1 on v0

v1 whole, which is shorter than its diff:
```python
import functools
import math

import jax
import jax.numpy as jnp
from jax import lax
from jax.experimental import pallas as pl
from jax.experimental.pallas import tpu as pltpu
from jax.sharding import PartitionSpec as P

LOG2E = math.log2(math.e)
TILE = 512
ROW_BLOCK = 512
CHUNKS = 4
NT = (((1,), (1,)), ((), ()))


def dots_kernel(coef, grad_ref, prev_ref, next_ref, bias_ref, total_ref, out_ref):
    @pl.when(pl.program_id(0) == 0)
    def _():
        out_ref[...] = total_ref[...]

    rows, width = grad_ref.shape
    block = min(ROW_BLOCK, rows)
    for top in range(0, rows, block):
        here = pl.ds(top, block)
        logits = lax.dot_general(
            prev_ref[here, :], next_ref[...], NT, preferred_element_type=jnp.float32
        )
        terms = grad_ref[here, :].astype(jnp.float32) * jnp.exp2(logits * coef - bias_ref[here, :])
        part = terms[:, :128]
        for left in range(128, width, 128):
            part = part + terms[:, left : left + 128]
        out_ref[here, :] += part


def grads_kernel(
    coef, pieces, grad_ref, prev_ref, prev_t_ref, next_ref, bias_ref, dot_ref, total_ref,
    out_ref, *rest
):
    piece_refs, held = rest[:-1], rest[-1]

    @pl.when(pl.program_id(0) == 0)
    def _():
        out_ref[...] = total_ref[...]

    rows = grad_ref.shape[0]
    block = min(ROW_BLOCK, rows)
    for top in range(0, rows, block):
        here = pl.ds(top, block)
        logits = lax.dot_general(
            prev_ref[here, :], next_ref[...], NT, preferred_element_type=jnp.float32
        )
        scaled = jnp.exp2(logits * coef - bias_ref[here, :])
        shifted = grad_ref[here, :].astype(jnp.float32) - dot_ref[here, :]
        dlogits = (scaled * shifted).astype(jnp.bfloat16)
        held[here, :] = dlogits
        out_ref[here, :] += jnp.dot(dlogits, next_ref[...], preferred_element_type=jnp.float32)
    flipped = jnp.dot(prev_t_ref[...], held[...], preferred_element_type=jnp.float32)
    for (start, size, kind), ref in zip(pieces, piece_refs):
        ref[...] = flipped[start : start + size, :].T.astype(kind)


def row_dots(grad, prev, nxt, bias, total, first, coef):
    rows, features = prev.shape
    columns = nxt.shape[0]
    tile = min(TILE, columns)
    offset = first // tile
    whole = lambda shape: pl.BlockSpec(shape, lambda j: (0, 0))
    return pl.pallas_call(
        functools.partial(dots_kernel, coef),
        grid=(columns // tile,),
        out_shape=jax.ShapeDtypeStruct(total.shape, jnp.float32),
        in_specs=[
            pl.BlockSpec((rows, tile), lambda j: (0, j + offset)),
            whole(prev.shape),
            pl.BlockSpec((tile, features), lambda j: (j, 0)),
            whole(bias.shape),
            whole(total.shape),
        ],
        out_specs=whole(total.shape),
        compiler_params=pltpu.CompilerParams(vmem_limit_bytes=48 << 20),
        cost_estimate=pl.CostEstimate(
            flops=2 * rows * columns * features,
            bytes_accessed=2 * rows * columns,
            transcendentals=rows * columns,
        ),
    )(grad, prev, nxt, bias, total)


def grad_terms(grad, prev, prev_t, nxt, bias, dots, total, first, coef, pieces):
    rows, features = prev.shape
    columns = nxt.shape[0]
    tile = min(TILE, columns)
    offset = first // tile
    whole = lambda shape: pl.BlockSpec(shape, lambda j: (0, 0))
    return pl.pallas_call(
        functools.partial(grads_kernel, coef, pieces),
        grid=(columns // tile,),
        out_shape=[jax.ShapeDtypeStruct(total.shape, jnp.float32)]
        + [jax.ShapeDtypeStruct((columns, size), kind) for _, size, kind in pieces],
        in_specs=[
            pl.BlockSpec((rows, tile), lambda j: (0, j + offset)),
            whole(prev.shape),
            whole(prev_t.shape),
            pl.BlockSpec((tile, features), lambda j: (j, 0)),
            whole(bias.shape),
            whole(dots.shape),
            whole(total.shape),
        ],
        out_specs=[whole(total.shape)]
        + [pl.BlockSpec((tile, size), lambda j: (j, 0)) for _, size, _ in pieces],
        scratch_shapes=[pltpu.VMEM((rows, tile), jnp.bfloat16)],
        compiler_params=pltpu.CompilerParams(vmem_limit_bytes=56 << 20),
        cost_estimate=pl.CostEstimate(
            flops=6 * rows * columns * features,
            bytes_accessed=2 * rows * columns,
            transcendentals=rows * columns,
        ),
    )(grad, prev, prev_t, nxt, bias, dots, total)


def body(cols, grid_rows, grad_table, prev_embed, next_embed, log_norm):
    rows, columns = grad_table.shape
    features = prev_embed.shape[1] * cols
    scale = 2.0 / math.sqrt(features)
    coef = scale * LOG2E
    share = next_embed.shape[1]
    paired = cols == 4 and grid_rows == 4 and share % 128 == 0
    step = columns // CHUNKS if columns % (CHUNKS * TILE) == 0 else columns
    starts = list(range(0, columns, step))
    r, c = lax.axis_index("row"), lax.axis_index("col")

    def swap(x, bit):
        return lax.ppermute(x, "row", [(i, i ^ bit) for i in range(grid_rows)])

    def shift(x, by):
        return lax.ppermute(x, "col", [(i, (i + by) % cols) for i in range(cols)])

    if paired:
        order = (0, 2, 1, 3)
        arrived = jnp.stack([prev_embed] + [shift(prev_embed, cols - a) for a in range(1, cols)])
        prev = jnp.concatenate(
            [
                lax.dynamic_index_in_dim(arrived, ((r ^ o) - c + cols) % cols, 0, keepdims=False)
                for o in order
            ],
            axis=1,
        )
        nexts = []
        for first in starts:
            mine = next_embed[first : first + step]
            across = swap(mine, 2)
            both = jnp.concatenate([mine, across], axis=1)
            nexts.append(jnp.concatenate([both, swap(both, 1)], axis=1))
        pieces = (
            (0, share, jnp.float32),
            (share, share, jnp.float32),
            (2 * share, 2 * share, jnp.bfloat16),
        )
    else:
        prev = lax.all_gather(prev_embed, "col", axis=1, tiled=True)
        gathered = lax.all_gather(next_embed, "row", axis=1, tiled=True)
        nexts = [gathered[first : first + step] for first in starts]
        pieces = ((0, features, jnp.float32),)

    bias = log_norm[:, None] * LOG2E
    total = jnp.zeros((rows, 128), jnp.float32)
    for first, nxt in zip(starts, nexts):
        total = row_dots(grad_table, prev, nxt, bias, total, first, coef)
    dots = lax.psum(jnp.sum(total, axis=1), "col")[:, None]

    prev_t = prev.T
    bias = bias - math.log2(scale)
    total = jnp.zeros((rows, features), jnp.float32)
    ends = []
    for first, nxt in zip(starts, nexts):
        total, *sums = grad_terms(
            grad_table, prev, prev_t, nxt, bias, dots, total, first, coef, pieces
        )
        if paired:
            own, far, give = sums
            got = swap(give, 1).astype(jnp.float32)
            far = swap((far + got[:, share:]).astype(jnp.bfloat16), 2)
            ends.append(own + got[:, :share] + far.astype(jnp.float32))
        else:
            ends.append(lax.psum_scatter(sums[0], "row", scatter_dimension=1, tiled=True))
    next_grad = jnp.concatenate(ends, axis=0)

    if paired:
        def block(col):
            code = jnp.bitwise_xor(col, r)
            place = jnp.where(code == 1, 2, jnp.where(code == 2, 1, code))
            return lax.dynamic_slice_in_dim(total, place * share, share, 1)

        prev_grad = block(c)
        for a in range(1, cols):
            away = block((c + a) % cols).astype(jnp.bfloat16)
            prev_grad = prev_grad + shift(away, a).astype(jnp.float32)
    else:
        prev_grad = lax.psum_scatter(total, "col", scatter_dimension=1, tiled=True)
    return (prev_grad, next_grad)


def solution(mesh):
    placed = (P(("parts", "row"), "col"), P("row", "col"), P("col", "row"), P(("parts", "row")))
    return jax.shard_map(
        functools.partial(body, mesh.shape["col"], mesh.shape["row"]),
        mesh=mesh,
        in_specs=placed,
        out_specs=(P(("parts", "row"), "col"), P(("parts", "col"), "row")),
        check_vma=False,
    )
```

time: 451 us -> 362 us (0.80)
  waiting for transfers between devices: 291 us -> 96.6 us
  Pallas kernels: 0 us -> 120 us
  matrix products: 94.5 us -> 0 us
  starting transfers between devices: 0.34 us -> 44.1 us
  blocking collectives: 6.97 us -> 41.2 us
  local copies, waits for them, and re-layouts: 0.01 us -> 23 us
  between operations: 13.8 us -> 1.02 us
  other arithmetic: 42.8 us -> 34.5 us
    reduce_scatter x2 -> x0, waiting for transfers between devices: 181 us -> none  [the longest x1 130 us: body(): lax.psum_scatter(next_terms, 'row', scatter_dimension=1, tiled=True)]
    pallas_call x0 -> x8, Pallas kernels: none -> 120 us  [the longest x4 88.6 us: grad_terms(): pl.pallas_call(functools.partial(grads_kernel, coef, pieces), grid=(colum...]
    all_gather x2 -> x0, waiting for transfers between devices: 108 us -> none  [the longest x1 61.1 us: body(): next_full = lax.all_gather(next_embed, 'row', axis=1, tiled=True)]
    ppermute x0 -> x22, waiting for transfers between devices: none -> 96.6 us  [the longest x6 56.5 us: shift(): return lax.ppermute(x, 'col', [(i, (i + by) % cols) for i in range(cols)])]
    dot_general x3 -> x0, matrix products: 94.5 us -> none  [the longest x1 42.8 us: body(): lax.dot_general(prev_full, next_full, (((1,), (1,)), ((), ())), preferred...]
    ppermute x0 -> x22, starting transfers between devices: none -> 44.1 us  [the longest x16 34.7 us: swap(): return lax.ppermute(x, 'row', [(i, i ^ bit) for i in range(grid_rows)])]
    convert_element_type x1 -> x8, other arithmetic: 42.8 us -> 2.46 us  [the longest x4 1.94 us: body(): got = swap(give, 1).astype(jnp.float32)]
    psum x1, blocking collectives: 6.97 us -> 41.2 us  [body(): dots = lax.psum(jnp.sum(total, axis=1), 'col')[:, None]]
  transfers between devices with their start and end apart: 4 -> 22, of which waited for: 4 -> 10; matrix products, arithmetic and copies ran while one was open for 6% -> 13% of each run, Pallas kernels for 0% -> 25%
where the time goes in v1:
time: 362 us; the launch traced here: 360 us
  Pallas kernels  120 us (33%)
  waiting for transfers between devices  96.6 us (27%)
  starting transfers between devices  44.1 us (12%)
  blocking collectives  41.2 us (11%)
  other arithmetic  34.5 us (10%)
  local copies, waits for them, and re-layouts  23 us (6%)
    pallas_call x4, Pallas kernels, grad_terms(): pl.pallas_call(functools.partial(grads_kernel, coef, pieces), grid=(colum...  88.6 us
    ppermute x6, waiting for transfers between devices, shift(): return lax.ppermute(x, 'col', [(i, (i + by) % cols) for i in range(cols)])  56.5 us
    psum x1, blocking collectives, body(): dots = lax.psum(jnp.sum(total, axis=1), 'col')[:, None]  41.2 us
    ppermute x16, waiting for transfers between devices, swap(): return lax.ppermute(x, 'row', [(i, i ^ bit) for i in range(grid_rows)])  40.1 us
    ppermute x16, starting transfers between devices, swap(): return lax.ppermute(x, 'row', [(i, i ^ bit) for i in range(grid_rows)])  34.7 us
    pallas_call x4, Pallas kernels, row_dots(): pl.pallas_call(functools.partial(dots_kernel, coef), grid=(columns // til...  31.2 us
    concatenate x4, other arithmetic, body(): nexts.append(jnp.concatenate([both, swap(both, 1)], axis=1))  12 us
    dynamic_slice x5, local copies, waits for them, and re-layouts, body(): lax.dynamic_index_in_dim(arrived, ((r ^ o) - c + cols) % cols, 0, keepdim...  9.53 us
  transfers between devices with their start and end apart: 22, of which 10 were waited for; matrix products, arithmetic and copies ran while one was open for 13% of the time, Pallas kernels for 25%

profile of v1, /device:TPU:9, one launch (start us, length us, event | category | flops | bytes accessed | tf_op | source)
XLA Modules:
  0.0 360.1 jit_solution(2442343158593065532)
XLA Ops:
  0.7 2.5 collective-permute-start.1
  3.2 2.2 collective-permute-start.2
  10.4 3.4 collective-permute-done
  15.0 21.8 %collective-permute-done.1 = bf16[2048,128]{1,0:T(8,128)(2,1)} collective-permute-done((bf16[2048,128]{1,0:T(8,128)(2,1)}, bf16[2048,128]{1,0:T(8,128)(2,1)}, u32[]{:S(2)}, u32[]{:S(2)}) %collective-permute-start.1) | collective-permute-done | bytes 524320 | tf_op jit(solution)/shard_map/ppermute | solution.py:138
  38.1 10.0 %collective-permute-done.2 = bf16[2048,128]{1,0:T(8,128)(2,1)} collective-permute-done((bf16[2048,128]{1,0:T(8,128)(2,1)}, bf16[2048,128]{1,0:T(8,128)(2,1)}, u32[]{:S(2)}, u32[]{:S(2)}) %collective-permute-start.2) | collective-permute-done | bytes 524320 | tf_op jit(solution)/shard_map/ppermute | solution.py:138
  67.7 2.6 fusion.8
  72.4 2.9 copy.37.prev_ref
  75.5 3.8 %pad_maximum_fusion.6.next_ref = bf16[2048,512]{1,0:T(8,128)(2,1)} fusion(bf16[2048,256]{1,0:T(8,128)(2,1)} %collective-permute-done.10, bf16[2048,128]{1,0:T(8,128)(2,1)} %collective-permute-done.9, bf16[2048,128]{1,0:T(8,128)(2,1)} %copy-done.8), kind=kLoop, calls=%fused_computation.6 | loop fusion | flops 6291456 | bytes 4194304 | tf_op jit(solution)/shard_map/concatenate | solution.py:155
  79.3 2.8 pad_maximum_fusion.5.next_ref
  82.2 7.8 %shard_map.59.total_ref = f32[2048,128]{1,0:T(8,128)S(1)} custom-call(bf16[2048,8192]{1,0:T(8,128)(2,1)} %grad_ref.15, bf16[2048,512]{1,0:T(8,128)(2,1)S(1)} %copy.37.prev_ref, bf16[2048,512]{1,0:T(8,128)(2,1)} %pad_maximum_fusion.6.next_ref, f32[2048,1]{1,0:T(8,128)S(1)} %copy.29.bias_ref, f32[2048,128]{1,0:T(8,128)S(1)} %broadcast_in_dim.10.total_ref), custom_call_target="tpu_custom_call" | custom-call | flops 4294967296 | bytes 8388608 | tf_op jit(solution)/shard_map/pallas_call | solution.py:70
  90.1 2.8 pad_maximum_fusion.4.next_ref
  92.9 7.8 %shard_map.60.total_ref = f32[2048,128]{1,0:T(8,128)S(1)} custom-call(bf16[2048,8192]{1,0:T(8,128)(2,1)} %grad_ref.15, bf16[2048,512]{1,0:T(8,128)(2,1)S(1)} %copy.37.prev_ref, bf16[2048,512]{1,0:T(8,128)(2,1)} %pad_maximum_fusion.5.next_ref, f32[2048,1]{1,0:T(8,128)S(1)} %copy.29.bias_ref, f32[2048,128]{1,0:T(8,128)S(1)} %shard_map.59.total_ref), custom_call_target="tpu_custom_call" | custom-call | flops 4294967296 | bytes 8388608 | tf_op jit(solution)/shard_map/pallas_call | solution.py:70
  100.7 7.8 %shard_map.61.total_ref = f32[2048,128]{1,0:T(8,128)S(1)} custom-call(bf16[2048,8192]{1,0:T(8,128)(2,1)} %grad_ref.15, bf16[2048,512]{1,0:T(8,128)(2,1)S(1)} %copy.37.prev_ref, bf16[2048,512]{1,0:T(8,128)(2,1)} %pad_maximum_fusion.4.next_ref, f32[2048,1]{1,0:T(8,128)S(1)} %copy.29.bias_ref, f32[2048,128]{1,0:T(8,128)S(1)} %shard_map.60.total_ref), custom_call_target="tpu_custom_call" | custom-call | flops 4294967296 | bytes 8388608 | tf_op jit(solution)/shard_map/pallas_call | solution.py:70
  108.5 2.6 pad_maximum_fusion.3.next_ref
  111.1 7.8 %shard_map.62 = f32[2048,128]{1,0:T(8,128)S(1)} custom-call(bf16[2048,8192]{1,0:T(8,128)(2,1)} %grad_ref.15, bf16[2048,512]{1,0:T(8,128)(2,1)S(1)} %copy.37.prev_ref, bf16[2048,512]{1,0:T(8,128)(2,1)} %pad_maximum_fusion.3.next_ref, f32[2048,1]{1,0:T(8,128)S(1)} %copy.29.bias_ref, f32[2048,128]{1,0:T(8,128)S(1)} %shard_map.61.total_ref), custom_call_target="tpu_custom_call" | custom-call | flops 4294967296 | bytes 8388608 | tf_op jit(solution)/shard_map/pallas_call | solution.py:70
  121.8 41.2 %psum.7.dot_ref = f32[2048,1]{1,0:T(8,128)} all-reduce(f32[2048,1]{1,0:T(8,128)S(1)} %copy.30), channel_id=1, replica_groups=mesh['parts'=2,'col'=4,'row'=4] {'col'}, use_global_device_ids=true, to_apply=%region_1.2 | all-reduce | flops 2048 | bytes 16384 | tf_op jit(solution)/shard_map/psum | solution.py:171
  163.0 2.5 broadcast_in_dim.12.total_ref
  165.5 21.2 %shard_map.63 = (f32[2048,512]{1,0:T(8,128)}, f32[2048,128]{1,0:T(8,128)}, f32[2048,128]{1,0:T(8,128)}, bf16[2048,256]{1,0:T(8,128)(2,1)}) custom-call(bf16[2048,8192]{1,0:T(8,128)(2,1)} %grad_ref.15, bf16[2048,512]{1,0:T(8,128)(2,1)} %copy-done, bf16[512,2048]{1,0:T(8,128)(2,1)} %get-tuple-element.41.prev_t_ref, ...), custom_call_target="tpu_custom_call" | custom-call | flops 12884901888 | bytes 8388608 | tf_op jit(solution)/shard_map/pallas_call | solution.py:97
  187.9 22.4 %shard_map.64 = (f32[2048,512]{1,0:T(8,128)}, f32[2048,128]{1,0:T(8,128)}, f32[2048,128]{1,0:T(8,128)}, bf16[2048,256]{1,0:T(8,128)(2,1)}) custom-call(bf16[2048,8192]{1,0:T(8,128)(2,1)} %grad_ref.15, bf16[2048,512]{1,0:T(8,128)(2,1)} %copy-done, bf16[512,2048]{1,0:T(8,128)(2,1)} %get-tuple-element.41.prev_t_ref, ...), custom_call_target="tpu_custom_call" | custom-call | flops 12884901888 | bytes 8388608 | tf_op jit(solution)/shard_map/pallas_call | solution.py:97
  210.3 22.4 %shard_map.65 = (f32[2048,512]{1,0:T(8,128)}, f32[2048,128]{1,0:T(8,128)}, f32[2048,128]{1,0:T(8,128)}, bf16[2048,256]{1,0:T(8,128)(2,1)}) custom-call(bf16[2048,8192]{1,0:T(8,128)(2,1)} %grad_ref.15, bf16[2048,512]{1,0:T(8,128)(2,1)} %copy-done, bf16[512,2048]{1,0:T(8,128)(2,1)} %get-tuple-element.41.prev_t_ref, ...), custom_call_target="tpu_custom_call" | custom-call | flops 12884901888 | bytes 8388608 | tf_op jit(solution)/shard_map/pallas_call | solution.py:97
  232.6 22.6 %shard_map.66 = (f32[2048,512]{1,0:T(8,128)}, f32[2048,128]{1,0:T(8,128)}, f32[2048,128]{1,0:T(8,128)}, bf16[2048,256]{1,0:T(8,128)(2,1)}) custom-call(bf16[2048,8192]{1,0:T(8,128)(2,1)} %grad_ref.15, bf16[2048,512]{1,0:T(8,128)(2,1)} %copy-done, bf16[512,2048]{1,0:T(8,128)(2,1)} %get-tuple-element.41.prev_t_ref, ...), custom_call_target="tpu_custom_call" | custom-call | flops 12884901888 | bytes 8388608 | tf_op jit(solution)/shard_map/pallas_call | solution.py:97
  257.4 2.5 collective-permute-start.11
  259.8 2.3 collective-permute-start.12
  262.7 9.6 %collective-permute-done.11 = bf16[2048,128]{1,0:T(8,128)(2,1)S(1)} collective-permute-done((bf16[2048,128]{1,0:T(8,128)(2,1)S(1)}, bf16[2048,128]{1,0:T(8,128)(2,1)S(1)}, u32[]{:S(2)}, u32[]{:S(2)}) %collective-permute-start.11) | collective-permute-done | bytes 524320 | tf_op jit(solution)/shard_map/ppermute | solution.py:138
  272.3 22.5 %collective-permute-start.18 = (bf16[2048,256]{1,0:T(8,128)(2,1)}, bf16[2048,256]{1,0:T(8,128)(2,1)S(1)}, u32[]{:S(2)}, u32[]{:S(2)}) collective-permute-start(bf16[2048,256]{1,0:T(8,128)(2,1)} %get-tuple-element.29), channel_id=1, source_target_pairs={{0,1},{1,0},{2,3},{3,2},{4,5},{5,4},{6,7},{7,6},{8,9},{9,8},{10,11... | collective-permute-start | bytes 3145736 | tf_op jit(solution)/shard_map/ppermute | solution.py:135
  294.7 10.1 %collective-permute-done.12 = bf16[2048,128]{1,0:T(8,128)(2,1)} collective-permute-done((bf16[2048,128]{1,0:T(8,128)(2,1)S(1)}, bf16[2048,128]{1,0:T(8,128)(2,1)}, u32[]{:S(2)}, u32[]{:S(2)}) %collective-permute-start.12) | collective-permute-done | bytes 524320 | tf_op jit(solution)/shard_map/ppermute | solution.py:138
  307.2 2.7 convert_add_fusion
  317.1 6.8 %collective-permute-done.15 = bf16[2048,128]{1,0:T(8,128)(2,1)S(1)} collective-permute-done((bf16[2048,128]{1,0:T(8,128)(2,1)S(1)}, bf16[2048,128]{1,0:T(8,128)(2,1)S(1)}, u32[]{:S(2)}, u32[]{:S(2)}) %collective-permute-start.15) | collective-permute-done | bytes 524320 | tf_op jit(solution)/shard_map/ppermute | solution.py:135
  324.2 11.0 %collective-permute-done.17 = bf16[2048,128]{1,0:T(8,128)(2,1)S(1)} collective-permute-done((bf16[2048,128]{1,0:T(8,128)(2,1)S(1)}, bf16[2048,128]{1,0:T(8,128)(2,1)S(1)}, u32[]{:S(2)}, u32[]{:S(2)}) %collective-permute-start.17) | collective-permute-done | bytes 524320 | tf_op jit(solution)/shard_map/ppermute | solution.py:135
  335.3 11.1 %collective-permute-done.19 = bf16[2048,128]{1,0:T(8,128)(2,1)S(1)} collective-permute-done((bf16[2048,128]{1,0:T(8,128)(2,1)S(1)}, bf16[2048,128]{1,0:T(8,128)(2,1)S(1)}, u32[]{:S(2)}, u32[]{:S(2)}) %collective-permute-start.19) | collective-permute-done | bytes 524320 | tf_op jit(solution)/shard_map/ppermute | solution.py:135
  346.6 11.1 %collective-permute-done.21 = bf16[2048,128]{1,0:T(8,128)(2,1)S(1)} collective-permute-done((bf16[2048,128]{1,0:T(8,128)(2,1)S(1)}, bf16[2048,128]{1,0:T(8,128)(2,1)S(1)}, u32[]{:S(2)}, u32[]{:S(2)}) %collective-permute-start.21) | collective-permute-done | bytes 524320 | tf_op jit(solution)/shard_map/ppermute | solution.py:135
  357.8 2.3 pad_maximum_fusion
  (104 shorter events, 46.2 us)
Async XLA Ops:
  0.6 8.0 %copy-start.21 = (f32[2048]{0:T(1024)S(1)}, f32[2048]{0:T(1024)}, u32[]{:S(2)}) copy-start(f32[2048]{0:T(1024)} %param.7) | copy-start | bytes 24580
  0.6 13.2 %collective-permute-start = (bf16[2048,128]{1,0:T(8,128)(2,1)}, bf16[2048,128]{1,0:T(8,128)(2,1)}, u32[]{:S(2)}, u32[]{:S(2)}) collective-permute-start(bf16[2048,128]{1,0:T(8,128)(2,1)} %param.5), channel_id=1, source_target_pairs={{0,12},{4,0},{8,4},{12,8},{1,13},{5,1},{9,5},{13,9},{2,14},{6,2},{... | collective-permute-start | bytes 1572872 | tf_op jit(solution)/shard_map/ppermute | solution.py:138
  0.7 36.2 %collective-permute-start.1 = (bf16[2048,128]{1,0:T(8,128)(2,1)}, bf16[2048,128]{1,0:T(8,128)(2,1)}, u32[]{:S(2)}, u32[]{:S(2)}) collective-permute-start(bf16[2048,128]{1,0:T(8,128)(2,1)} %param.5), channel_id=1, source_target_pairs={{0,8},{4,12},{8,0},{12,4},{1,9},{5,13},{9,1},{13,5},{2,10},{6,14},... | collective-permute-start | bytes 1572872 | tf_op jit(solution)/shard_map/ppermute | solution.py:138
  3.2 44.9 %collective-permute-start.2 = (bf16[2048,128]{1,0:T(8,128)(2,1)}, bf16[2048,128]{1,0:T(8,128)(2,1)}, u32[]{:S(2)}, u32[]{:S(2)}) collective-permute-start(bf16[2048,128]{1,0:T(8,128)(2,1)} %param.5), channel_id=1, source_target_pairs={{0,4},{4,8},{8,12},{12,0},{1,5},{5,9},{9,13},{13,1},{2,6},{6,10},{... | collective-permute-start | bytes 1572872 | tf_op jit(solution)/shard_map/ppermute | solution.py:138
  7.0 52.4 %copy-start.8 = (bf16[2048,128]{1,0:T(8,128)(2,1)}, bf16[2048,128]{1,0:T(8,128)(2,1)S(1)}, u32[]{:S(2)}) copy-start(bf16[2048,128]{1,0:T(8,128)(2,1)S(1)} %get-tuple-element.37) | copy-start | bytes 1572868
  7.0 55.9 %copy-start.6 = (bf16[2048,128]{1,0:T(8,128)(2,1)}, bf16[2048,128]{1,0:T(8,128)(2,1)S(1)}, u32[]{:S(2)}) copy-start(bf16[2048,128]{1,0:T(8,128)(2,1)S(1)} %get-tuple-element.40) | copy-start | bytes 1572868
  7.0 58.2 %copy-start.4 = (bf16[2048,128]{1,0:T(8,128)(2,1)}, bf16[2048,128]{1,0:T(8,128)(2,1)S(1)}, u32[]{:S(2)}) copy-start(bf16[2048,128]{1,0:T(8,128)(2,1)S(1)} %get-tuple-element.38) | copy-start | bytes 1572868
  7.1 63.2 %copy-start.2 = (bf16[2048,128]{1,0:T(8,128)(2,1)}, bf16[2048,128]{1,0:T(8,128)(2,1)S(1)}, u32[]{:S(2)}) copy-start(bf16[2048,128]{1,0:T(8,128)(2,1)S(1)} %get-tuple-element.39) | copy-start | bytes 1572868
  7.1 52.4 %collective-permute-start.9 = (bf16[2048,128]{1,0:T(8,128)(2,1)S(1)}, bf16[2048,128]{1,0:T(8,128)(2,1)}, u32[]{:S(2)}, u32[]{:S(2)}) collective-permute-start(bf16[2048,128]{1,0:T(8,128)(2,1)S(1)} %get-tuple-element.37), channel_id=1, source_target_pairs={{0,2},{1,3},{2,0},{3,1},{4,6},{5,7},{6,4},{7,5},{8,10},{9,11},{10,... | collective-permute-start | bytes 1572872 | tf_op jit(solution)/shard_map/ppermute | solution.py:135
  8.3 54.6 %collective-permute-start.7 = (bf16[2048,128]{1,0:T(8,128)(2,1)S(1)}, bf16[2048,128]{1,0:T(8,128)(2,1)}, u32[]{:S(2)}, u32[]{:S(2)}) collective-permute-start(bf16[2048,128]{1,0:T(8,128)(2,1)S(1)} %get-tuple-element.40), channel_id=1, source_target_pairs={{0,2},{1,3},{2,0},{3,1},{4,6},{5,7},{6,4},{7,5},{8,10},{9,11},{10,... | collective-permute-start | bytes 1572872 | tf_op jit(solution)/shard_map/ppermute | solution.py:135
  13.8 51.4 %collective-permute-start.5 = (bf16[2048,128]{1,0:T(8,128)(2,1)S(1)}, bf16[2048,128]{1,0:T(8,128)(2,1)}, u32[]{:S(2)}, u32[]{:S(2)}) collective-permute-start(bf16[2048,128]{1,0:T(8,128)(2,1)S(1)} %get-tuple-element.38), channel_id=1, source_target_pairs={{0,2},{1,3},{2,0},{3,1},{4,6},{5,7},{6,4},{7,5},{8,10},{9,11},{10,... | collective-permute-start | bytes 1572872 | tf_op jit(solution)/shard_map/ppermute | solution.py:135
  36.9 33.4 %collective-permute-start.3 = (bf16[2048,128]{1,0:T(8,128)(2,1)S(1)}, bf16[2048,128]{1,0:T(8,128)(2,1)}, u32[]{:S(2)}, u32[]{:S(2)}) collective-permute-start(bf16[2048,128]{1,0:T(8,128)(2,1)S(1)} %get-tuple-element.39), channel_id=1, source_target_pairs={{0,2},{1,3},{2,0},{3,1},{4,6},{5,7},{6,4},{7,5},{8,10},{9,11},{10,... | collective-permute-start | bytes 1572872 | tf_op jit(solution)/shard_map/ppermute | solution.py:135
  61.6 13.9 %collective-permute-start.10 = (bf16[2048,256]{1,0:T(8,128)(2,1)}, bf16[2048,256]{1,0:T(8,128)(2,1)}, u32[]{:S(2)}, u32[]{:S(2)}) collective-permute-start(bf16[2048,256]{1,0:T(8,128)(2,1)} %pad_maximum_fusion.10), channel_id=1, source_target_pairs={{0,1},{1,0},{2,3},{3,2},{4,5},{5,4},{6,7},{7,6},{8,9},{9,8},{10,11... | collective-permute-start | bytes 3145736 | tf_op jit(solution)/shard_map/ppermute | solution.py:135
  65.0 14.3 %collective-permute-start.8 = (bf16[2048,256]{1,0:T(8,128)(2,1)}, bf16[2048,256]{1,0:T(8,128)(2,1)}, u32[]{:S(2)}, u32[]{:S(2)}) collective-permute-start(bf16[2048,256]{1,0:T(8,128)(2,1)} %pad_maximum_fusion.9), channel_id=1, source_target_pairs={{0,1},{1,0},{2,3},{3,2},{4,5},{5,4},{6,7},{7,6},{8,9},{9,8},{10,11... | collective-permute-start | bytes 3145736 | tf_op jit(solution)/shard_map/ppermute | solution.py:135
  67.3 22.7 %collective-permute-start.6 = (bf16[2048,256]{1,0:T(8,128)(2,1)}, bf16[2048,256]{1,0:T(8,128)(2,1)}, u32[]{:S(2)}, u32[]{:S(2)}) collective-permute-start(bf16[2048,256]{1,0:T(8,128)(2,1)} %pad_maximum_fusion.8), channel_id=1, source_target_pairs={{0,1},{1,0},{2,3},{3,2},{4,5},{5,4},{6,7},{7,6},{8,9},{9,8},{10,11... | collective-permute-start | bytes 3145736 | tf_op jit(solution)/shard_map/ppermute | solution.py:135
  75.3 35.8 %copy-start = (bf16[2048,512]{1,0:T(8,128)(2,1)}, bf16[2048,512]{1,0:T(8,128)(2,1)S(1)}, u32[]{:S(2)}) copy-start(bf16[2048,512]{1,0:T(8,128)(2,1)S(1)} %copy.37.prev_ref) | copy-start | bytes 6291460
  75.3 33.2 %collective-permute-start.4 = (bf16[2048,256]{1,0:T(8,128)(2,1)}, bf16[2048,256]{1,0:T(8,128)(2,1)S(1)}, u32[]{:S(2)}, u32[]{:S(2)}) collective-permute-start(bf16[2048,256]{1,0:T(8,128)(2,1)} %pad_maximum_fusion.7), channel_id=1, source_target_pairs={{0,1},{1,0},{2,3},{3,2},{4,5},{5,4},{6,7},{7,6},{8,9},{9,8},{10,11... | collective-permute-start | bytes 3145736 | tf_op jit(solution)/shard_map/ppermute | solution.py:135
  186.7 123.2 %collective-permute-start.14 = (bf16[2048,256]{1,0:T(8,128)(2,1)}, bf16[2048,256]{1,0:T(8,128)(2,1)S(1)}, u32[]{:S(2)}, u32[]{:S(2)}) collective-permute-start(bf16[2048,256]{1,0:T(8,128)(2,1)} %get-tuple-element.23), channel_id=1, source_target_pairs={{0,1},{1,0},{2,3},{3,2},{4,5},{5,4},{6,7},{7,6},{8,9},{9,8},{10,11... | collective-permute-start | bytes 3145736 | tf_op jit(solution)/shard_map/ppermute | solution.py:135
  257.4 14.9 %collective-permute-start.11 = (bf16[2048,128]{1,0:T(8,128)(2,1)S(1)}, bf16[2048,128]{1,0:T(8,128)(2,1)S(1)}, u32[]{:S(2)}, u32[]{:S(2)}) collective-permute-start(bf16[2048,128]{1,0:T(8,128)(2,1)S(1)} %get-tuple-element.34), channel_id=1, source_target_pairs={{0,4},{4,8},{8,12},{12,0},{1,5},{5,9},{9,13},{13,1},{2,6},{6,10},{... | collective-permute-start | bytes 1572872 | tf_op jit(solution)/shard_map/ppermute | solution.py:138
  259.8 45.0 %collective-permute-start.12 = (bf16[2048,128]{1,0:T(8,128)(2,1)S(1)}, bf16[2048,128]{1,0:T(8,128)(2,1)}, u32[]{:S(2)}, u32[]{:S(2)}) collective-permute-start(bf16[2048,128]{1,0:T(8,128)(2,1)S(1)} %get-tuple-element.36), channel_id=1, source_target_pairs={{0,8},{4,12},{8,0},{12,4},{1,9},{5,13},{9,1},{13,5},{2,10},{6,14},... | collective-permute-start | bytes 1572872 | tf_op jit(solution)/shard_map/ppermute | solution.py:138
  262.1 45.1 %collective-permute-start.13 = (bf16[2048,128]{1,0:T(8,128)(2,1)S(1)}, bf16[2048,128]{1,0:T(8,128)(2,1)}, u32[]{:S(2)}, u32[]{:S(2)}) collective-permute-start(bf16[2048,128]{1,0:T(8,128)(2,1)S(1)} %get-tuple-element.35), channel_id=1, source_target_pairs={{0,12},{4,0},{8,4},{12,8},{1,13},{5,1},{9,5},{13,9},{2,14},{6,2},{... | collective-permute-start | bytes 1572872 | tf_op jit(solution)/shard_map/ppermute | solution.py:138
  262.1 49.3 %collective-permute-start.16 = (bf16[2048,256]{1,0:T(8,128)(2,1)}, bf16[2048,256]{1,0:T(8,128)(2,1)}, u32[]{:S(2)}, u32[]{:S(2)}) collective-permute-start(bf16[2048,256]{1,0:T(8,128)(2,1)} %get-tuple-element.26), channel_id=1, source_target_pairs={{0,1},{1,0},{2,3},{3,2},{4,5},{5,4},{6,7},{7,6},{8,9},{9,8},{10,11... | collective-permute-start | bytes 3145736 | tf_op jit(solution)/shard_map/ppermute | solution.py:135
  272.3 42.2 %collective-permute-start.18 = (bf16[2048,256]{1,0:T(8,128)(2,1)}, bf16[2048,256]{1,0:T(8,128)(2,1)S(1)}, u32[]{:S(2)}, u32[]{:S(2)}) collective-permute-start(bf16[2048,256]{1,0:T(8,128)(2,1)} %get-tuple-element.29), channel_id=1, source_target_pairs={{0,1},{1,0},{2,3},{3,2},{4,5},{5,4},{6,7},{7,6},{8,9},{9,8},{10,11... | collective-permute-start | bytes 3145736 | tf_op jit(solution)/shard_map/ppermute | solution.py:135
  304.8 10.9 %collective-permute-start.20 = (bf16[2048,256]{1,0:T(8,128)(2,1)}, bf16[2048,256]{1,0:T(8,128)(2,1)S(1)}, u32[]{:S(2)}, u32[]{:S(2)}) collective-permute-start(bf16[2048,256]{1,0:T(8,128)(2,1)} %get-tuple-element.32), channel_id=1, source_target_pairs={{0,1},{1,0},{2,3},{3,2},{4,5},{5,4},{6,7},{7,6},{8,9},{9,8},{10,11... | collective-permute-start | bytes 3145736 | tf_op jit(solution)/shard_map/ppermute | solution.py:135
  311.3 12.7 %collective-permute-start.15 = (bf16[2048,128]{1,0:T(8,128)(2,1)S(1)}, bf16[2048,128]{1,0:T(8,128)(2,1)S(1)}, u32[]{:S(2)}, u32[]{:S(2)}) collective-permute-start(bf16[2048,128]{1,0:T(8,128)(2,1)S(1)} %fusion.6), channel_id=1, source_target_pairs={{0,2},{1,3},{2,0},{3,1},{4,6},{5,7},{6,4},{7,5},{8,10},{9,11},{10,... | collective-permute-start | bytes 1572872 | tf_op jit(solution)/shard_map/ppermute | solution.py:135
  313.1 22.1 %collective-permute-start.17 = (bf16[2048,128]{1,0:T(8,128)(2,1)S(1)}, bf16[2048,128]{1,0:T(8,128)(2,1)S(1)}, u32[]{:S(2)}, u32[]{:S(2)}) collective-permute-start(bf16[2048,128]{1,0:T(8,128)(2,1)S(1)} %fusion.4), channel_id=1, source_target_pairs={{0,2},{1,3},{2,0},{3,1},{4,6},{5,7},{6,4},{7,5},{8,10},{9,11},{10,... | collective-permute-start | bytes 1572872 | tf_op jit(solution)/shard_map/ppermute | solution.py:135
  314.7 31.7 %collective-permute-start.19 = (bf16[2048,128]{1,0:T(8,128)(2,1)S(1)}, bf16[2048,128]{1,0:T(8,128)(2,1)S(1)}, u32[]{:S(2)}, u32[]{:S(2)}) collective-permute-start(bf16[2048,128]{1,0:T(8,128)(2,1)S(1)} %fusion.2), channel_id=1, source_target_pairs={{0,2},{1,3},{2,0},{3,1},{4,6},{5,7},{6,4},{7,5},{8,10},{9,11},{10,... | collective-permute-start | bytes 1572872 | tf_op jit(solution)/shard_map/ppermute | solution.py:135
  315.9 8.0 %copy-start.14 = (f32[2048,128]{1,0:T(8,128)S(1)}, f32[2048,128]{1,0:T(8,128)}, u32[]{:S(2)}) copy-start(f32[2048,128]{1,0:T(8,128)} %get-tuple-element.22) | copy-start | bytes 3145732
  316.1 19.1 %copy-start.16 = (f32[2048,128]{1,0:T(8,128)S(1)}, f32[2048,128]{1,0:T(8,128)}, u32[]{:S(2)}) copy-start(f32[2048,128]{1,0:T(8,128)} %get-tuple-element.25) | copy-start | bytes 3145732
  316.1 41.6 %collective-permute-start.21 = (bf16[2048,128]{1,0:T(8,128)(2,1)S(1)}, bf16[2048,128]{1,0:T(8,128)(2,1)S(1)}, u32[]{:S(2)}, u32[]{:S(2)}) collective-permute-start(bf16[2048,128]{1,0:T(8,128)(2,1)S(1)} %fusion), channel_id=1, source_target_pairs={{0,2},{1,3},{2,0},{3,1},{4,6},{5,7},{6,4},{7,5},{8,10},{9,11},{10,... | collective-permute-start | bytes 1572872 | tf_op jit(solution)/shard_map/ppermute | solution.py:135
  324.1 22.3 %copy-start.15 = (f32[2048,128]{1,0:T(8,128)S(1)}, f32[2048,128]{1,0:T(8,128)}, u32[]{:S(2)}) copy-start(f32[2048,128]{1,0:T(8,128)} %get-tuple-element.28) | copy-start | bytes 3145732
  335.3 22.3 %copy-start.13 = (f32[2048,128]{1,0:T(8,128)S(1)}, f32[2048,128]{1,0:T(8,128)}, u32[]{:S(2)}) copy-start(f32[2048,128]{1,0:T(8,128)} %get-tuple-element.31) | copy-start | bytes 3145732
  (12 other events, 50.8 us)

commit v2 on v1

v2 whole, which is shorter than its diff:
```python
import functools
import math

import jax
import jax.numpy as jnp
from jax import lax
from jax.experimental import pallas as pl
from jax.experimental.pallas import tpu as pltpu
from jax.sharding import PartitionSpec as P

LOG2E = math.log2(math.e)
TILE = 512
ROW_BLOCK = 512
CHUNKS = 4
NT = (((1,), (1,)), ((), ()))


def arrange_kernel(places_ref, arrived_ref, prev_ref, prev_t_ref):
    block = arrived_ref[0, 0]
    prev_ref[...] = block
    prev_t_ref[...] = block.T


def arrange(arrived, places):
    blocks, halves, height, share = arrived.shape
    rows, features = halves * height, blocks * share
    return pl.pallas_call(
        arrange_kernel,
        grid_spec=pltpu.PrefetchScalarGridSpec(
            num_scalar_prefetch=1,
            grid=(blocks, halves),
            in_specs=[
                pl.BlockSpec(
                    (1, 1, height, share),
                    lambda i, h, places: (places[i], places[blocks + h], 0, 0),
                )
            ],
            out_specs=[
                pl.BlockSpec((height, share), lambda i, h, places: (h, i)),
                pl.BlockSpec((share, height), lambda i, h, places: (i, h)),
            ],
        ),
        out_shape=[
            jax.ShapeDtypeStruct((rows, features), arrived.dtype),
            jax.ShapeDtypeStruct((features, rows), arrived.dtype),
        ],
        cost_estimate=pl.CostEstimate(
            flops=0, bytes_accessed=6 * rows * features, transcendentals=0
        ),
    )(places, arrived)


def join(next_refs, held):
    left = 0
    for ref in next_refs:
        held[:, left : left + ref.shape[1]] = ref[...]
        left += ref.shape[1]


def dots_kernel(coef, count, grad_ref, prev_ref, bias_ref, total_ref, *rest):
    next_refs, (out_ref, next_held) = rest[:count], rest[count:]

    @pl.when(pl.program_id(0) == 0)
    def _():
        out_ref[...] = total_ref[...]

    join(next_refs, next_held)
    rows, width = grad_ref.shape
    block = min(ROW_BLOCK, rows)
    for top in range(0, rows, block):
        here = pl.ds(top, block)
        logits = lax.dot_general(
            prev_ref[here, :], next_held[...], NT, preferred_element_type=jnp.float32
        )
        terms = grad_ref[here, :].astype(jnp.float32) * jnp.exp2(logits * coef - bias_ref[here, :])
        part = terms[:, :128]
        for left in range(128, width, 128):
            part = part + terms[:, left : left + 128]
        out_ref[here, :] += part


def grads_kernel(
    coef, pieces, count, grad_ref, prev_ref, prev_t_ref, bias_ref, dot_ref, total_ref, *rest
):
    next_refs = rest[:count]
    out_ref, *piece_refs = rest[count:-2]
    next_held, held = rest[-2:]

    @pl.when(pl.program_id(0) == 0)
    def _():
        out_ref[...] = total_ref[...]

    join(next_refs, next_held)
    rows = grad_ref.shape[0]
    block = min(ROW_BLOCK, rows)
    for top in range(0, rows, block):
        here = pl.ds(top, block)
        logits = lax.dot_general(
            prev_ref[here, :], next_held[...], NT, preferred_element_type=jnp.float32
        )
        scaled = jnp.exp2(logits * coef - bias_ref[here, :])
        shifted = grad_ref[here, :].astype(jnp.float32) - dot_ref[here, :]
        dlogits = (scaled * shifted).astype(jnp.bfloat16)
        held[here, :] = dlogits
        out_ref[here, :] += jnp.dot(dlogits, next_held[...], preferred_element_type=jnp.float32)
    flipped = jnp.dot(prev_t_ref[...], held[...], preferred_element_type=jnp.float32)
    for (start, size, kind), ref in zip(pieces, piece_refs):
        ref[...] = flipped[start : start + size, :].T.astype(kind)


def whole(shape):
    return pl.BlockSpec(shape, lambda j: (0, 0))


def tiles_of(tile, nexts):
    return [
        pl.BlockSpec((tile, x.shape[1]), functools.partial(lambda skip, j: (j + skip, 0), at // tile))
        for x, at in nexts
    ]


def row_dots(grad, prev, nexts, bias, total, first, step, coef):
    rows, features = prev.shape
    tile = min(TILE, step)
    offset = first // tile
    return pl.pallas_call(
        functools.partial(dots_kernel, coef, len(nexts)),
        grid=(step // tile,),
        out_shape=jax.ShapeDtypeStruct(total.shape, jnp.float32),
        in_specs=[
            pl.BlockSpec((rows, tile), lambda j: (0, j + offset)),
            whole(prev.shape),
            whole(bias.shape),
            whole(total.shape),
        ]
        + tiles_of(tile, nexts),
        out_specs=whole(total.shape),
        scratch_shapes=[pltpu.VMEM((tile, features), jnp.bfloat16)],
        compiler_params=pltpu.CompilerParams(vmem_limit_bytes=48 << 20),
        cost_estimate=pl.CostEstimate(
            flops=2 * rows * step * features,
            bytes_accessed=2 * rows * step,
            transcendentals=rows * step,
        ),
    )(grad, prev, bias, total, *[x for x, _ in nexts])


def grad_terms(grad, prev, prev_t, nexts, bias, dots, total, first, step, coef, pieces):
    rows, features = prev.shape
    tile = min(TILE, step)
    offset = first // tile
    return pl.pallas_call(
        functools.partial(grads_kernel, coef, pieces, len(nexts)),
        grid=(step // tile,),
        out_shape=[jax.ShapeDtypeStruct(total.shape, jnp.float32)]
        + [jax.ShapeDtypeStruct((step, size), kind) for _, size, kind in pieces],
        in_specs=[
            pl.BlockSpec((rows, tile), lambda j: (0, j + offset)),
            whole(prev.shape),
            whole(prev_t.shape),
            whole(bias.shape),
            whole(dots.shape),
            whole(total.shape),
        ]
        + tiles_of(tile, nexts),
        out_specs=[whole(total.shape)]
        + [pl.BlockSpec((tile, size), lambda j: (j, 0)) for _, size, _ in pieces],
        scratch_shapes=[
            pltpu.VMEM((tile, features), jnp.bfloat16),
            pltpu.VMEM((rows, tile), jnp.bfloat16),
        ],
        compiler_params=pltpu.CompilerParams(vmem_limit_bytes=56 << 20),
        cost_estimate=pl.CostEstimate(
            flops=6 * rows * step * features,
            bytes_accessed=2 * rows * step,
            transcendentals=rows * step,
        ),
    )(grad, prev, prev_t, bias, dots, total, *[x for x, _ in nexts])


def body(parts, cols, grid_rows, grad_table, prev_embed, next_embed, log_norm):
    rows, columns = grad_table.shape
    features = prev_embed.shape[1] * cols
    scale = 2.0 / math.sqrt(features)
    coef = scale * LOG2E
    share = next_embed.shape[1]
    paired = parts == 2 and cols == 4 and grid_rows == 4 and share % 128 == 0
    step = columns // CHUNKS if columns % (CHUNKS * TILE) == 0 else columns
    starts = list(range(0, columns, step))
    r, c, p = lax.axis_index("row"), lax.axis_index("col"), lax.axis_index("parts")

    def swap(x, bit):
        return lax.ppermute(x, "row", [(i, i ^ bit) for i in range(grid_rows)])

    def shift(x, by):
        return lax.ppermute(x, "col", [(i, (i + by) % cols) for i in range(cols)])

    def trade(x):
        return lax.ppermute(x, "parts", [(0, 1), (1, 0)])

    if paired:
        half = rows // 2
        mine = lax.dynamic_slice_in_dim(prev_embed, p * half, half, 0)
        other = lax.dynamic_slice_in_dim(prev_embed, (1 - p) * half, half, 0)
        arrived = [mine, other]
        for a in range(1, cols):
            near = shift(mine, cols - a)
            arrived += [near, trade(near)]
        beside = swap(next_embed, 1)
        across = [swap(next_embed[first : first + step], 2) for first in starts]
        corner = [swap(x, 1) for x in across]
        nexts = [
            [(next_embed, first), (x, 0), (beside, first), (y, 0)]
            for first, x, y in zip(starts, across, corner)
        ]
        places = [((r ^ o) - c + cols) % cols for o in (0, 2, 1, 3)] + [p, 1 - p]
        arrived = jnp.stack(arrived).reshape(cols, 2, half, share)
        prev, prev_t = arrange(arrived, jnp.stack(places).astype(jnp.int32))
        pieces = (
            (0, share, jnp.float32),
            (share, share, jnp.float32),
            (2 * share, 2 * share, jnp.bfloat16),
        )
    else:
        prev = lax.all_gather(prev_embed, "col", axis=1, tiled=True)
        prev_t = prev.T
        gathered = lax.all_gather(next_embed, "row", axis=1, tiled=True)
        nexts = [[(gathered, first)] for first in starts]
        pieces = ((0, features, jnp.float32),)

    bias = log_norm[:, None] * LOG2E
    total = jnp.zeros((rows, 128), jnp.float32)
    for first, nxt in zip(starts, nexts):
        total = row_dots(grad_table, prev, nxt, bias, total, first, step, coef)
    dots = jnp.sum(total, axis=1)
    if paired:
        mine = dots.reshape(rows // 128, 128)
        dots = (mine + sum(shift(mine, a) for a in range(1, cols))).reshape(rows)
    else:
        dots = lax.psum(dots, "col")
    dots = dots[:, None]

    bias = bias - math.log2(scale)
    total = jnp.zeros((rows, features), jnp.float32)
    ends, sent = [], []
    for k, (first, nxt) in enumerate(zip(starts, nexts)):
        if paired and k >= 2:
            total, sent[k - 2] = lax.optimization_barrier((total, sent[k - 2]))
        if paired and k >= 3:
            total, ends[k - 3] = lax.optimization_barrier((total, ends[k - 3]))
        total, *sums = grad_terms(
            grad_table, prev, prev_t, nxt, bias, dots, total, first, step, coef, pieces
        )
        if paired:
            own, far, give = sums
            got = swap(give, 1)
            sent.append((far + got[:, share:].astype(jnp.float32)).astype(jnp.bfloat16))
            ends.append(own + got[:, :share].astype(jnp.float32))
            if k >= 1:
                ends[k - 1] = ends[k - 1] + swap(sent[k - 1], 2).astype(jnp.float32)
        else:
            ends.append(lax.psum_scatter(sums[0], "row", scatter_dimension=1, tiled=True))
    if paired:
        ends[-1] = ends[-1] + swap(sent[-1], 2).astype(jnp.float32)
    next_grad = jnp.concatenate(ends, axis=0)

    if paired:
        def block(col):
            code = jnp.bitwise_xor(col, r)
            place = jnp.where(code == 1, 2, jnp.where(code == 2, 1, code))
            return lax.dynamic_slice_in_dim(total, place * share, share, 1)

        prev_grad = block(c)
        for a in range(1, cols):
            away = block((c + a) % cols).astype(jnp.bfloat16)
            prev_grad = prev_grad + shift(away, a).astype(jnp.float32)
    else:
        prev_grad = lax.psum_scatter(total, "col", scatter_dimension=1, tiled=True)
    return (prev_grad, next_grad)


def solution(mesh):
    placed = (P(("parts", "row"), "col"), P("row", "col"), P("col", "row"), P(("parts", "row")))
    return jax.shard_map(
        functools.partial(body, *(mesh.shape[axis] for axis in ("parts", "col", "row"))),
        mesh=mesh,
        in_specs=placed,
        out_specs=(P(("parts", "row"), "col"), P(("parts", "col"), "row")),
        check_vma=False,
    )
```

time: 362 us -> 278 us (0.77)
  blocking collectives: 41.2 us -> 0 us
  other arithmetic: 34.5 us -> 9.07 us
  waiting for transfers between devices: 96.6 us -> 75.1 us
  Pallas kernels: 120 us -> 131 us
  local copies, waits for them, and re-layouts: 23 us -> 18.7 us
    psum x1 -> x0, blocking collectives: 41.2 us -> none  [body(): dots = lax.psum(jnp.sum(total, axis=1), 'col')[:, None]]
    ppermute x16 -> x17, waiting for transfers between devices: 40.1 us -> 15.4 us  [swap(): return lax.ppermute(x, 'row', [(i, i ^ bit) for i in range(grid_rows)])]
    concatenate x8 -> x0, other arithmetic: 20.5 us -> none  [the longest x4 12 us: body(): nexts.append(jnp.concatenate([both, swap(both, 1)], axis=1))]
    pallas_call x8 -> x9, Pallas kernels: 120 us -> 131 us  [the longest x4 89.8 us: grad_terms(): pl.pallas_call(functools.partial(grads_kernel, coef, pieces, len(nexts)),...]
    ppermute x16 -> x17, starting transfers between devices: 34.7 us -> 24.1 us  [swap(): return lax.ppermute(x, 'row', [(i, i ^ bit) for i in range(grid_rows)])]
    dynamic_slice x5 -> x0, local copies, waits for them, and re-layouts: 9.53 us -> none  [body(): lax.dynamic_index_in_dim(arrived, ((r ^ o) - c + cols) % cols, 0, keepdim...]
    ppermute x0 -> x3, waiting for transfers between devices: none -> 6.64 us  [trade(): return lax.ppermute(x, 'parts', [(0, 1), (1, 0)])]
    ppermute x6 -> x9, starting transfers between devices: 9.46 us -> 14.9 us  [shift(): return lax.ppermute(x, 'col', [(i, (i + by) % cols) for i in range(cols)])]
  transfers between devices with their start and end apart: 22 -> 29, of which waited for: 10 -> 11; matrix products, arithmetic and copies ran while one was open for 13% -> 7% of each run, Pallas kernels for 25% -> 28%
where the time goes in v2:
time: 278 us; the launch traced here: 277 us
  Pallas kernels  131 us (47%)
  waiting for transfers between devices  75.1 us (27%)
  starting transfers between devices  41.8 us (15%)
  local copies, waits for them, and re-layouts  18.7 us (7%)
  other arithmetic  9.07 us (3%)
    pallas_call x4, Pallas kernels, grad_terms(): pl.pallas_call(functools.partial(grads_kernel, coef, pieces, len(nexts)),...  89.8 us
    ppermute x9, waiting for transfers between devices, shift(): return lax.ppermute(x, 'col', [(i, (i + by) % cols) for i in range(cols)])  53 us
    pallas_call x4, Pallas kernels, row_dots(): pl.pallas_call(functools.partial(dots_kernel, coef, len(nexts)), grid=(st...  34.5 us
    ppermute x17, starting transfers between devices, swap(): return lax.ppermute(x, 'row', [(i, i ^ bit) for i in range(grid_rows)])  24.1 us
    ppermute x17, waiting for transfers between devices, swap(): return lax.ppermute(x, 'row', [(i, i ^ bit) for i in range(grid_rows)])  15.4 us
    ppermute x9, starting transfers between devices, shift(): return lax.ppermute(x, 'col', [(i, (i + by) % cols) for i in range(cols)])  14.9 us
    pallas_call x1, Pallas kernels, arrange(): pl.pallas_call(arrange_kernel, grid_spec=pltpu.PrefetchScalarGridSpec(num...  6.93 us
    unnamed x35, local copies, waits for them, and re-layouts  6.88 us
  transfers between devices with their start and end apart: 29, of which 11 were waited for; matrix products, arithmetic and copies ran while one was open for 7% of the time, Pallas kernels for 28%

profile of v2, /device:TPU:9, one launch (start us, length us, event | category | flops | bytes accessed | tf_op | source)
XLA Modules:
  0.0 276.7 jit_solution(11448918953180116853)
XLA Ops:
  2.4 2.5 collective-permute-start.2
  4.8 2.2 collective-permute-start.4
  8.6 2.7 fusion
  16.3 5.1 %collective-permute-done.2 = bf16[1024,128]{1,0:T(8,128)(2,1)S(1)} collective-permute-done((bf16[1024,128]{1,0:T(8,128)(2,1)S(1)}, bf16[1024,128]{1,0:T(8,128)(2,1)S(1)}, u32[]{:S(2)}, u32[]{:S(2)}) %collective-permute-start.2) | collective-permute-done | bytes 262176 | tf_op jit(solution)/shard_map/ppermute | solution.py:196
  22.6 4.4 %collective-permute-done.4 = bf16[1024,128]{1,0:T(8,128)(2,1)S(1)} collective-permute-done((bf16[1024,128]{1,0:T(8,128)(2,1)S(1)}, bf16[1024,128]{1,0:T(8,128)(2,1)S(1)}, u32[]{:S(2)}, u32[]{:S(2)}) %collective-permute-start.4) | collective-permute-done | bytes 262176 | tf_op jit(solution)/shard_map/ppermute | solution.py:196
  29.9 3.0 %collective-permute-done.3 = bf16[1024,128]{1,0:T(8,128)(2,1)S(1)} collective-permute-done((bf16[1024,128]{1,0:T(8,128)(2,1)S(1)}, bf16[1024,128]{1,0:T(8,128)(2,1)S(1)}, u32[]{:S(2)}, u32[]{:S(2)}) %collective-permute-start.3) | collective-permute-done | bytes 262176 | tf_op jit(solution)/shard_map/ppermute | solution.py:199
  32.9 1.9 collective-permute-start.11
  34.8 3.6 %collective-permute-done.5 = bf16[1024,128]{1,0:T(8,128)(2,1)S(1)} collective-permute-done((bf16[1024,128]{1,0:T(8,128)(2,1)S(1)}, bf16[1024,128]{1,0:T(8,128)(2,1)S(1)}, u32[]{:S(2)}, u32[]{:S(2)}) %collective-permute-start.5) | collective-permute-done | bytes 262176 | tf_op jit(solution)/shard_map/ppermute | solution.py:199
  38.4 1.9 collective-permute-start.13
  40.3 2.5 collective-permute-start.8
  45.0 6.9 %shard_map.59 = (bf16[2048,512]{1,0:T(8,128)(2,1)}, bf16[512,2048]{1,0:T(8,128)(2,1)}) custom-call(s32[6]{0:T(128)} %stack.54.places_ref, bf16[4,2,1024,128]{3,2,1,0:T(8,128)(2,1)} %bitcast.28), custom_call_target="tpu_custom_call" | custom-call | bytes 6291456 | tf_op jit(solution)/shard_map/pallas_call | solution.py:27
  54.4 5.2 %collective-permute-start.14 = (bf16[2048,128]{1,0:T(8,128)(2,1)S(1)}, bf16[2048,128]{1,0:T(8,128)(2,1)S(1)}, u32[]{:S(2)}, u32[]{:S(2)}) collective-permute-start(bf16[2048,128]{1,0:T(8,128)(2,1)S(1)} %collective-permute-done.13.rest_1_), channel_id=1, source_target_pairs={{0,1},{1,0},{2,3},{3,2},{4,5},{5,4},{6,7},{7,6},{8,9},{9,8},{10,11... | collective-permute-start | bytes 1572872 | tf_op jit(solution)/shard_map/ppermute | solution.py:193
  59.6 8.6 %shard_map.60.total_ref = f32[2048,128]{1,0:T(8,128)S(1)} custom-call(bf16[2048,8192]{1,0:T(8,128)(2,1)} %grad_ref.15, bf16[2048,512]{1,0:T(8,128)(2,1)} %get-tuple-element.24.prev_ref, f32[2048,1]{1,0:T(8,128)S(1)} %copy.9.bias_ref, f32[2048,128]{1,0:T(8,128)S(1)} %broadcast_in_dim.7.total_ref, bf16[8192,128]{1,0:T(8,128)(2,1)} %rest_0_.15, ...), custom_call_target="tpu_custom_call" | custom-call | flops 4294967296 | bytes 8388608 | tf_op jit(solution)/shard_map/pallas_call | solution.py:126
  68.2 8.7 %shard_map.61.total_ref = f32[2048,128]{1,0:T(8,128)S(1)} custom-call(bf16[2048,8192]{1,0:T(8,128)(2,1)} %grad_ref.15, bf16[2048,512]{1,0:T(8,128)(2,1)} %get-tuple-element.24.prev_ref, f32[2048,1]{1,0:T(8,128)S(1)} %copy.9.bias_ref, f32[2048,128]{1,0:T(8,128)S(1)} %shard_map.60.total_ref, bf16[8192,128]{1,0:T(8,128)(2,1)} %rest_0_.15, ...), custom_call_target="tpu_custom_call" | custom-call | flops 4294967296 | bytes 8388608 | tf_op jit(solution)/shard_map/pallas_call | solution.py:126
  77.0 8.7 %shard_map.62.total_ref = f32[2048,128]{1,0:T(8,128)S(1)} custom-call(bf16[2048,8192]{1,0:T(8,128)(2,1)} %grad_ref.15, bf16[2048,512]{1,0:T(8,128)(2,1)} %get-tuple-element.24.prev_ref, f32[2048,1]{1,0:T(8,128)S(1)} %copy.9.bias_ref, f32[2048,128]{1,0:T(8,128)S(1)} %shard_map.61.total_ref, bf16[8192,128]{1,0:T(8,128)(2,1)} %rest_0_.15, ...), custom_call_target="tpu_custom_call" | custom-call | flops 4294967296 | bytes 8388608 | tf_op jit(solution)/shard_map/pallas_call | solution.py:126
  85.7 8.5 %shard_map.63 = f32[2048,128]{1,0:T(8,128)S(1)} custom-call(bf16[2048,8192]{1,0:T(8,128)(2,1)} %grad_ref.15, bf16[2048,512]{1,0:T(8,128)(2,1)} %get-tuple-element.24.prev_ref, f32[2048,1]{1,0:T(8,128)S(1)} %copy.9.bias_ref, f32[2048,128]{1,0:T(8,128)S(1)} %shard_map.62.total_ref, bf16[8192,128]{1,0:T(8,128)(2,1)} %rest_0_.15, ...), custom_call_target="tpu_custom_call" | custom-call | flops 4294967296 | bytes 8388608 | tf_op jit(solution)/shard_map/pallas_call | solution.py:126
  95.3 3.2 %collective-permute-start.15 = (f32[16,128]{1,0:T(8,128)S(1)}, f32[16,128]{1,0:T(8,128)S(1)}, u32[]{:S(2)}, u32[]{:S(2)}) collective-permute-start(f32[16,128]{1,0:T(8,128)S(1)} %bitcast.31), channel_id=1, source_target_pairs={{0,4},{4,8},{8,12},{12,0},{1,5},{5,9},{9,13},{13,1},{2,6},{6,10},{... | collective-permute-start | bytes 24584 | tf_op jit(solution)/shard_map/ppermute | solution.py:196
  98.5 4.0 %collective-permute-start.16 = (f32[16,128]{1,0:T(8,128)S(1)}, f32[16,128]{1,0:T(8,128)S(1)}, u32[]{:S(2)}, u32[]{:S(2)}) collective-permute-start(f32[16,128]{1,0:T(8,128)S(1)} %bitcast.32), channel_id=1, source_target_pairs={{0,8},{4,12},{8,0},{12,4},{1,9},{5,13},{9,1},{13,5},{2,10},{6,14},... | collective-permute-start | bytes 24584 | tf_op jit(solution)/shard_map/ppermute | solution.py:196
  106.4 2.5 broadcast_in_dim.8.total_ref
  109.0 21.5 %shard_map.64 = (f32[2048,512]{1,0:T(8,128)}, f32[2048,128]{1,0:T(8,128)}, f32[2048,128]{1,0:T(8,128)}, bf16[2048,256]{1,0:T(8,128)(2,1)}) custom-call(bf16[2048,8192]{1,0:T(8,128)(2,1)} %grad_ref.15, bf16[2048,512]{1,0:T(8,128)(2,1)} %get-tuple-element.24.prev_ref, bf16[512,2048]{1,0:T(8,128)(2,1)} %get-tuple-element.25.prev_t_ref, ...), custom_call_target="tpu_custom_call" | custom-call | flops 12884901888 | bytes 8388608 | tf_op jit(solution)/shard_map/pallas_call | solution.py:152
  130.4 22.7 %shard_map.65 = (f32[2048,512]{1,0:T(8,128)}, f32[2048,128]{1,0:T(8,128)}, f32[2048,128]{1,0:T(8,128)}, bf16[2048,256]{1,0:T(8,128)(2,1)}) custom-call(bf16[2048,8192]{1,0:T(8,128)(2,1)} %grad_ref.15, bf16[2048,512]{1,0:T(8,128)(2,1)} %get-tuple-element.24.prev_ref, bf16[512,2048]{1,0:T(8,128)(2,1)} %get-tuple-element.25.prev_t_ref, ...), custom_call_target="tpu_custom_call" | custom-call | flops 12884901888 | bytes 8388608 | tf_op jit(solution)/shard_map/pallas_call | solution.py:152
  155.1 2.4 collective-permute-done.19
  157.5 2.1 add_convert_fusion.2
  161.3 22.7 %shard_map.66 = (f32[2048,512]{1,0:T(8,128)}, f32[2048,128]{1,0:T(8,128)}, f32[2048,128]{1,0:T(8,128)}, bf16[2048,256]{1,0:T(8,128)(2,1)}) custom-call(bf16[2048,8192]{1,0:T(8,128)(2,1)} %grad_ref.15, bf16[2048,512]{1,0:T(8,128)(2,1)} %get-tuple-element.24.prev_ref, bf16[512,2048]{1,0:T(8,128)(2,1)} %get-tuple-element.25.prev_t_ref, ...), custom_call_target="tpu_custom_call" | custom-call | flops 12884901888 | bytes 8388608 | tf_op jit(solution)/shard_map/pallas_call | solution.py:152
  185.1 23.0 %shard_map.67 = (f32[2048,512]{1,0:T(8,128)}, f32[2048,128]{1,0:T(8,128)}, f32[2048,128]{1,0:T(8,128)}, bf16[2048,256]{1,0:T(8,128)(2,1)}) custom-call(bf16[2048,8192]{1,0:T(8,128)(2,1)} %grad_ref.15, bf16[2048,512]{1,0:T(8,128)(2,1)} %get-tuple-element.24.prev_ref, bf16[512,2048]{1,0:T(8,128)(2,1)} %get-tuple-element.25.prev_t_ref, ...), custom_call_target="tpu_custom_call" | custom-call | flops 12884901888 | bytes 8388608 | tf_op jit(solution)/shard_map/pallas_call | solution.py:152
  208.6 2.1 dynamic-slice_convert_fusion.2
  216.3 7.8 %collective-permute-done.21 = bf16[2048,128]{1,0:T(8,128)(2,1)S(1)} collective-permute-done((bf16[2048,128]{1,0:T(8,128)(2,1)S(1)}, bf16[2048,128]{1,0:T(8,128)(2,1)S(1)}, u32[]{:S(2)}, u32[]{:S(2)}) %collective-permute-start.21) | collective-permute-done | bytes 524320 | tf_op jit(solution)/shard_map/ppermute | solution.py:196
  224.1 31.8 %collective-permute-done.22 = bf16[2048,128]{1,0:T(8,128)(2,1)S(1)} collective-permute-done((bf16[2048,128]{1,0:T(8,128)(2,1)S(1)}, bf16[2048,128]{1,0:T(8,128)(2,1)S(1)}, u32[]{:S(2)}, u32[]{:S(2)}) %collective-permute-start.22) | collective-permute-done | bytes 524320 | tf_op jit(solution)/shard_map/ppermute | solution.py:196
  255.9 2.8 %collective-permute-done.23 = bf16[2048,128]{1,0:T(8,128)(2,1)S(1)} collective-permute-done((bf16[2048,128]{1,0:T(8,128)(2,1)S(1)}, bf16[2048,128]{1,0:T(8,128)(2,1)S(1)}, u32[]{:S(2)}, u32[]{:S(2)}) %collective-permute-start.23) | collective-permute-done | bytes 524320 | tf_op jit(solution)/shard_map/ppermute | solution.py:196
  258.7 2.4 convert_add_fusion.3
  262.7 11.6 %collective-permute-done.28 = bf16[2048,128]{1,0:T(8,128)(2,1)S(1)} collective-permute-done((bf16[2048,128]{1,0:T(8,128)(2,1)S(1)}, bf16[2048,128]{1,0:T(8,128)(2,1)S(1)}, u32[]{:S(2)}, u32[]{:S(2)}) %collective-permute-start.28) | collective-permute-done | bytes 524320 | tf_op jit(solution)/shard_map/ppermute | solution.py:193
  274.5 2.3 pad_maximum_fusion
  (92 shorter events, 34.5 us)
Async XLA Ops:
  2.4 10.1 %collective-permute-start = (bf16[1024,128]{1,0:T(8,128)(2,1)S(1)}, bf16[1024,128]{1,0:T(8,128)(2,1)S(1)}, u32[]{:S(2)}, u32[]{:S(2)}) collective-permute-start(bf16[1024,128]{1,0:T(8,128)(2,1)S(1)} %get-tuple-element.47), channel_id=1, source_target_pairs={{0,12},{4,0},{8,4},{12,8},{1,13},{5,1},{9,5},{13,9},{2,14},{6,2},{... | collective-permute-start | bytes 786440 | tf_op jit(solution)/shard_map/ppermute | solution.py:196
  2.4 19.0 %collective-permute-start.2 = (bf16[1024,128]{1,0:T(8,128)(2,1)S(1)}, bf16[1024,128]{1,0:T(8,128)(2,1)S(1)}, u32[]{:S(2)}, u32[]{:S(2)}) collective-permute-start(bf16[1024,128]{1,0:T(8,128)(2,1)S(1)} %get-tuple-element.47), channel_id=1, source_target_pairs={{0,8},{4,12},{8,0},{12,4},{1,9},{5,13},{9,1},{13,5},{2,10},{6,14},... | collective-permute-start | bytes 786440 | tf_op jit(solution)/shard_map/ppermute | solution.py:196
  4.8 22.1 %collective-permute-start.4 = (bf16[1024,128]{1,0:T(8,128)(2,1)S(1)}, bf16[1024,128]{1,0:T(8,128)(2,1)S(1)}, u32[]{:S(2)}, u32[]{:S(2)}) collective-permute-start(bf16[1024,128]{1,0:T(8,128)(2,1)S(1)} %get-tuple-element.47), channel_id=1, source_target_pairs={{0,4},{4,8},{8,12},{12,0},{1,5},{5,9},{9,13},{13,1},{2,6},{6,10},{... | collective-permute-start | bytes 786440 | tf_op jit(solution)/shard_map/ppermute | solution.py:196
  7.0 52.5 %collective-permute-start.7 = (bf16[8192,128]{1,0:T(8,128)(2,1)}, bf16[8192,128]{1,0:T(8,128)(2,1)}, u32[]{:S(2)}, u32[]{:S(2)}) collective-permute-start(bf16[8192,128]{1,0:T(8,128)(2,1)} %rest_0_.15), channel_id=1, source_target_pairs={{0,1},{1,0},{2,3},{3,2},{4,5},{5,4},{6,7},{7,6},{8,9},{9,8},{10,11... | collective-permute-start | bytes 6291464 | tf_op jit(solution)/shard_map/ppermute | solution.py:193
  11.3 29.1 %collective-permute-start.6 = (bf16[2048,128]{1,0:T(8,128)(2,1)}, bf16[2048,128]{1,0:T(8,128)(2,1)S(1)}, u32[]{:S(2)}, u32[]{:S(2)}) collective-permute-start(bf16[2048,128]{1,0:T(8,128)(2,1)} %get-tuple-element.54), channel_id=1, source_target_pairs={{0,2},{1,3},{2,0},{3,1},{4,6},{5,7},{6,4},{7,5},{8,10},{9,11},{10,... | collective-permute-start | bytes 1572872 | tf_op jit(solution)/shard_map/ppermute | solution.py:193
  12.5 15.7 %collective-permute-start.1 = (bf16[1024,128]{1,0:T(8,128)(2,1)S(1)}, bf16[1024,128]{1,0:T(8,128)(2,1)S(1)}, u32[]{:S(2)}, u32[]{:S(2)}) collective-permute-start(bf16[1024,128]{1,0:T(8,128)(2,1)S(1)} %collective-permute-done), channel_id=1, source_target_pairs={{0,16},{16,0},{1,17},{17,1},{2,18},{18,2},{3,19},{19,3},{4,20},{20... | collective-permute-start | bytes 786440 | tf_op jit(solution)/shard_map/ppermute | solution.py:199
  21.4 22.9 %collective-permute-start.9 = (bf16[2048,128]{1,0:T(8,128)(2,1)}, bf16[2048,128]{1,0:T(8,128)(2,1)}, u32[]{:S(2)}, u32[]{:S(2)}) collective-permute-start(bf16[2048,128]{1,0:T(8,128)(2,1)} %get-tuple-element.53), channel_id=1, source_target_pairs={{0,2},{1,3},{2,0},{3,1},{4,6},{5,7},{6,4},{7,5},{8,10},{9,11},{10,... | collective-permute-start | bytes 1572872 | tf_op jit(solution)/shard_map/ppermute | solution.py:193
  27.0 5.9 %collective-permute-start.3 = (bf16[1024,128]{1,0:T(8,128)(2,1)S(1)}, bf16[1024,128]{1,0:T(8,128)(2,1)S(1)}, u32[]{:S(2)}, u32[]{:S(2)}) collective-permute-start(bf16[1024,128]{1,0:T(8,128)(2,1)S(1)} %collective-permute-done.2), channel_id=1, source_target_pairs={{0,16},{16,0},{1,17},{17,1},{2,18},{18,2},{3,19},{19,3},{4,20},{20... | collective-permute-start | bytes 786440 | tf_op jit(solution)/shard_map/ppermute | solution.py:199
  28.2 10.2 %collective-permute-start.5 = (bf16[1024,128]{1,0:T(8,128)(2,1)S(1)}, bf16[1024,128]{1,0:T(8,128)(2,1)S(1)}, u32[]{:S(2)}, u32[]{:S(2)}) collective-permute-start(bf16[1024,128]{1,0:T(8,128)(2,1)S(1)} %collective-permute-done.4), channel_id=1, source_target_pairs={{0,16},{16,0},{1,17},{17,1},{2,18},{18,2},{3,19},{19,3},{4,20},{20... | collective-permute-start | bytes 786440 | tf_op jit(solution)/shard_map/ppermute | solution.py:199
  32.9 19.1 %collective-permute-start.11 = (bf16[2048,128]{1,0:T(8,128)(2,1)S(1)}, bf16[2048,128]{1,0:T(8,128)(2,1)S(1)}, u32[]{:S(2)}, u32[]{:S(2)}) collective-permute-start(bf16[2048,128]{1,0:T(8,128)(2,1)S(1)} %get-tuple-element.52), channel_id=1, source_target_pairs={{0,2},{1,3},{2,0},{3,1},{4,6},{5,7},{6,4},{7,5},{8,10},{9,11},{10,... | collective-permute-start | bytes 1572872 | tf_op jit(solution)/shard_map/ppermute | solution.py:193
  38.4 15.9 %collective-permute-start.13 = (bf16[2048,128]{1,0:T(8,128)(2,1)}, bf16[2048,128]{1,0:T(8,128)(2,1)S(1)}, u32[]{:S(2)}, u32[]{:S(2)}) collective-permute-start(bf16[2048,128]{1,0:T(8,128)(2,1)} %get-tuple-element.51), channel_id=1, source_target_pairs={{0,2},{1,3},{2,0},{3,1},{4,6},{5,7},{6,4},{7,5},{8,10},{9,11},{10,... | collective-permute-start | bytes 1572872 | tf_op jit(solution)/shard_map/ppermute | solution.py:193
  40.3 19.2 %collective-permute-start.8 = (bf16[2048,128]{1,0:T(8,128)(2,1)S(1)}, bf16[2048,128]{1,0:T(8,128)(2,1)}, u32[]{:S(2)}, u32[]{:S(2)}) collective-permute-start(bf16[2048,128]{1,0:T(8,128)(2,1)S(1)} %collective-permute-done.6.rest_1_), channel_id=1, source_target_pairs={{0,1},{1,0},{2,3},{3,2},{4,5},{5,4},{6,7},{7,6},{8,9},{9,8},{10,11... | collective-permute-start | bytes 1572872 | tf_op jit(solution)/shard_map/ppermute | solution.py:193
  44.3 23.9 %collective-permute-start.10 = (bf16[2048,128]{1,0:T(8,128)(2,1)}, bf16[2048,128]{1,0:T(8,128)(2,1)}, u32[]{:S(2)}, u32[]{:S(2)}) collective-permute-start(bf16[2048,128]{1,0:T(8,128)(2,1)} %collective-permute-done.9.rest_1_), channel_id=1, source_target_pairs={{0,1},{1,0},{2,3},{3,2},{4,5},{5,4},{6,7},{7,6},{8,9},{9,8},{10,11... | collective-permute-start | bytes 1572872 | tf_op jit(solution)/shard_map/ppermute | solution.py:193
  52.0 25.0 %collective-permute-start.12 = (bf16[2048,128]{1,0:T(8,128)(2,1)S(1)}, bf16[2048,128]{1,0:T(8,128)(2,1)S(1)}, u32[]{:S(2)}, u32[]{:S(2)}) collective-permute-start(bf16[2048,128]{1,0:T(8,128)(2,1)S(1)} %collective-permute-done.11.rest_1_), channel_id=1, source_target_pairs={{0,1},{1,0},{2,3},{3,2},{4,5},{5,4},{6,7},{7,6},{8,9},{9,8},{10,11... | collective-permute-start | bytes 1572872 | tf_op jit(solution)/shard_map/ppermute | solution.py:193
  54.4 31.3 %copy-start = (bf16[2048,128]{1,0:T(8,128)(2,1)}, bf16[2048,128]{1,0:T(8,128)(2,1)S(1)}, u32[]{:S(2)}) copy-start(bf16[2048,128]{1,0:T(8,128)(2,1)S(1)} %collective-permute-done.13.rest_1_) | copy-start | bytes 1572868
  54.4 31.3 %collective-permute-start.14 = (bf16[2048,128]{1,0:T(8,128)(2,1)S(1)}, bf16[2048,128]{1,0:T(8,128)(2,1)S(1)}, u32[]{:S(2)}, u32[]{:S(2)}) collective-permute-start(bf16[2048,128]{1,0:T(8,128)(2,1)S(1)} %collective-permute-done.13.rest_1_), channel_id=1, source_target_pairs={{0,1},{1,0},{2,3},{3,2},{4,5},{5,4},{6,7},{7,6},{8,9},{9,8},{10,11... | collective-permute-start | bytes 1572872 | tf_op jit(solution)/shard_map/ppermute | solution.py:193
  95.3 8.6 %collective-permute-start.15 = (f32[16,128]{1,0:T(8,128)S(1)}, f32[16,128]{1,0:T(8,128)S(1)}, u32[]{:S(2)}, u32[]{:S(2)}) collective-permute-start(f32[16,128]{1,0:T(8,128)S(1)} %bitcast.31), channel_id=1, source_target_pairs={{0,4},{4,8},{8,12},{12,0},{1,5},{5,9},{9,13},{13,1},{2,6},{6,10},{... | collective-permute-start | bytes 24584 | tf_op jit(solution)/shard_map/ppermute | solution.py:196
  98.5 5.4 %collective-permute-start.16 = (f32[16,128]{1,0:T(8,128)S(1)}, f32[16,128]{1,0:T(8,128)S(1)}, u32[]{:S(2)}, u32[]{:S(2)}) collective-permute-start(f32[16,128]{1,0:T(8,128)S(1)} %bitcast.32), channel_id=1, source_target_pairs={{0,8},{4,12},{8,0},{12,4},{1,9},{5,13},{9,1},{13,5},{2,10},{6,14},... | collective-permute-start | bytes 24584 | tf_op jit(solution)/shard_map/ppermute | solution.py:196
  102.5 2.5 collective-permute-start.17
  153.1 4.4 %collective-permute-start.19 = (bf16[2048,256]{1,0:T(8,128)(2,1)}, bf16[2048,256]{1,0:T(8,128)(2,1)S(1)}, u32[]{:S(2)}, u32[]{:S(2)}) collective-permute-start(bf16[2048,256]{1,0:T(8,128)(2,1)} %get-tuple-element.33), channel_id=1, source_target_pairs={{0,1},{1,0},{2,3},{3,2},{4,5},{5,4},{6,7},{7,6},{8,9},{9,8},{10,11... | collective-permute-start | bytes 3145736 | tf_op jit(solution)/shard_map/ppermute | solution.py:193
  155.0 5.8 %collective-permute-start.18 = (bf16[2048,256]{1,0:T(8,128)(2,1)}, bf16[2048,256]{1,0:T(8,128)(2,1)S(1)}, u32[]{:S(2)}, u32[]{:S(2)}) collective-permute-start(bf16[2048,256]{1,0:T(8,128)(2,1)} %get-tuple-element.29), channel_id=1, source_target_pairs={{0,1},{1,0},{2,3},{3,2},{4,5},{5,4},{6,7},{7,6},{8,9},{9,8},{10,11... | collective-permute-start | bytes 3145736 | tf_op jit(solution)/shard_map/ppermute | solution.py:193
  159.6 53.0 %collective-permute-start.24 = (bf16[2048,128]{1,0:T(8,128)(2,1)}, bf16[2048,128]{1,0:T(8,128)(2,1)}, u32[]{:S(2)}, u32[]{:S(2)}) collective-permute-start(bf16[2048,128]{1,0:T(8,128)(2,1)} %add_convert_fusion.2), channel_id=1, source_target_pairs={{0,2},{1,3},{2,0},{3,1},{4,6},{5,7},{6,4},{7,5},{8,10},{9,11},{10,... | collective-permute-start | bytes 1572872 | tf_op jit(solution)/shard_map/ppermute | solution.py:193
  160.9 24.0 %collective-permute-start.20 = (bf16[2048,128]{1,0:T(8,128)(2,1)S(1)}, bf16[2048,128]{1,0:T(8,128)(2,1)S(1)}, u32[]{:S(2)}, u32[]{:S(2)}) collective-permute-start(bf16[2048,128]{1,0:T(8,128)(2,1)S(1)} %add_convert_fusion.3), channel_id=1, source_target_pairs={{0,2},{1,3},{2,0},{3,1},{4,6},{5,7},{6,4},{7,5},{8,10},{9,11},{10,... | collective-permute-start | bytes 1572872 | tf_op jit(solution)/shard_map/ppermute | solution.py:193
  183.9 31.0 %collective-permute-start.25 = (bf16[2048,256]{1,0:T(8,128)(2,1)}, bf16[2048,256]{1,0:T(8,128)(2,1)S(1)}, u32[]{:S(2)}, u32[]{:S(2)}) collective-permute-start(bf16[2048,256]{1,0:T(8,128)(2,1)} %get-tuple-element.41), channel_id=1, source_target_pairs={{0,1},{1,0},{2,3},{3,2},{4,5},{5,4},{6,7},{7,6},{8,9},{9,8},{10,11... | collective-permute-start | bytes 3145736 | tf_op jit(solution)/shard_map/ppermute | solution.py:193
  208.1 53.0 %collective-permute-start.27 = (bf16[2048,256]{1,0:T(8,128)(2,1)}, bf16[2048,256]{1,0:T(8,128)(2,1)S(1)}, u32[]{:S(2)}, u32[]{:S(2)}) collective-permute-start(bf16[2048,256]{1,0:T(8,128)(2,1)} %get-tuple-element.44), channel_id=1, source_target_pairs={{0,1},{1,0},{2,3},{3,2},{4,5},{5,4},{6,7},{7,6},{8,9},{9,8},{10,11... | collective-permute-start | bytes 3145736 | tf_op jit(solution)/shard_map/ppermute | solution.py:193
  210.7 13.4 %collective-permute-start.21 = (bf16[2048,128]{1,0:T(8,128)(2,1)S(1)}, bf16[2048,128]{1,0:T(8,128)(2,1)S(1)}, u32[]{:S(2)}, u32[]{:S(2)}) collective-permute-start(bf16[2048,128]{1,0:T(8,128)(2,1)S(1)} %get-tuple-element.48), channel_id=1, source_target_pairs={{0,4},{4,8},{8,12},{12,0},{1,5},{5,9},{9,13},{13,1},{2,6},{6,10},{... | collective-permute-start | bytes 1572872 | tf_op jit(solution)/shard_map/ppermute | solution.py:196
  210.8 45.1 %collective-permute-start.22 = (bf16[2048,128]{1,0:T(8,128)(2,1)S(1)}, bf16[2048,128]{1,0:T(8,128)(2,1)S(1)}, u32[]{:S(2)}, u32[]{:S(2)}) collective-permute-start(bf16[2048,128]{1,0:T(8,128)(2,1)S(1)} %get-tuple-element.50), channel_id=1, source_target_pairs={{0,8},{4,12},{8,0},{12,4},{1,9},{5,13},{9,1},{13,5},{2,10},{6,14},... | collective-permute-start | bytes 1572872 | tf_op jit(solution)/shard_map/ppermute | solution.py:196
  212.6 46.1 %collective-permute-start.23 = (bf16[2048,128]{1,0:T(8,128)(2,1)S(1)}, bf16[2048,128]{1,0:T(8,128)(2,1)S(1)}, u32[]{:S(2)}, u32[]{:S(2)}) collective-permute-start(bf16[2048,128]{1,0:T(8,128)(2,1)S(1)} %get-tuple-element.49), channel_id=1, source_target_pairs={{0,12},{4,0},{8,4},{12,8},{1,13},{5,1},{9,5},{13,9},{2,14},{6,2},{... | collective-permute-start | bytes 1572872 | tf_op jit(solution)/shard_map/ppermute | solution.py:196
  215.0 46.1 %copy-start.10 = (f32[2048,128]{1,0:T(8,128)S(1)}, f32[2048,128]{1,0:T(8,128)}, u32[]{:S(2)}) copy-start(f32[2048,128]{1,0:T(8,128)} %get-tuple-element.45) | copy-start | bytes 3145732
  215.1 47.5 %copy-start.7 = (f32[2048,128]{1,0:T(8,128)S(1)}, f32[2048,128]{1,0:T(8,128)}, u32[]{:S(2)}) copy-start(f32[2048,128]{1,0:T(8,128)} %get-tuple-element.40) | copy-start | bytes 3145732
  215.1 47.5 %collective-permute-start.26 = (bf16[2048,128]{1,0:T(8,128)(2,1)S(1)}, bf16[2048,128]{1,0:T(8,128)(2,1)S(1)}, u32[]{:S(2)}, u32[]{:S(2)}) collective-permute-start(bf16[2048,128]{1,0:T(8,128)(2,1)S(1)} %add_convert_fusion.1), channel_id=1, source_target_pairs={{0,2},{1,3},{2,0},{3,1},{4,6},{5,7},{6,4},{7,5},{8,10},{9,11},{10,... | collective-permute-start | bytes 1572872 | tf_op jit(solution)/shard_map/ppermute | solution.py:193
  261.2 13.1 %collective-permute-start.28 = (bf16[2048,128]{1,0:T(8,128)(2,1)S(1)}, bf16[2048,128]{1,0:T(8,128)(2,1)S(1)}, u32[]{:S(2)}, u32[]{:S(2)}) collective-permute-start(bf16[2048,128]{1,0:T(8,128)(2,1)S(1)} %add_convert_fusion), channel_id=1, source_target_pairs={{0,2},{1,3},{2,0},{3,1},{4,6},{5,7},{6,4},{7,5},{8,10},{9,11},{10,... | collective-permute-start | bytes 1572872 | tf_op jit(solution)/shard_map/ppermute | solution.py:193
  (11 other events, 129.7 us)

commit v3 on v2

--- a/solution.py
+++ b/solution.py
@@ -80,10 +80,10 @@
 
 
 def grads_kernel(
-    coef, pieces, count, grad_ref, prev_ref, prev_t_ref, bias_ref, dot_ref, total_ref, *rest
+    coef, pieces, count, carried, grad_ref, prev_ref, prev_t_ref, bias_ref, dot_ref, total_ref, *rest
 ):
     next_refs = rest[:count]
-    out_ref, *piece_refs = rest[count:-2]
+    out_ref, *piece_refs = rest[count + carried : -2]
     next_held, held = rest[-2:]
 
     @pl.when(pl.program_id(0) == 0)
@@ -105,7 +105,10 @@
         out_ref[here, :] += jnp.dot(dlogits, next_held[...], preferred_element_type=jnp.float32)
     flipped = jnp.dot(prev_t_ref[...], held[...], preferred_element_type=jnp.float32)
     for (start, size, kind), ref in zip(pieces, piece_refs):
-        ref[...] = flipped[start : start + size, :].T.astype(kind)
+        value = flipped[start : start + size, :].T
+        if carried:
+            value = value + rest[count][:, start : start + size]
+        ref[...] = value.astype(kind)
 
 
 def whole(shape):
@@ -145,25 +148,32 @@
     )(grad, prev, bias, total, *[x for x, _ in nexts])
 
 
-def grad_terms(grad, prev, prev_t, nexts, bias, dots, total, first, step, coef, pieces):
-    rows, features = prev.shape
+def grad_terms(
+    grad, prev, prev_t, nexts, bias, dots, total, first, step, coef, pieces,
+    carry=(), split=1, part=0,
+):
+    features = prev.shape[1]
+    rows = prev.shape[0] // split
     tile = min(TILE, step)
     offset = first // tile
+    tall = lambda width: pl.BlockSpec((rows, width), lambda j: (part, 0))
+    shape = (rows, features)
     return pl.pallas_call(
-        functools.partial(grads_kernel, coef, pieces, len(nexts)),
+        functools.partial(grads_kernel, coef, pieces, len(nexts), len(carry)),
         grid=(step // tile,),
-        out_shape=[jax.ShapeDtypeStruct(total.shape, jnp.float32)]
+        out_shape=[jax.ShapeDtypeStruct(shape, jnp.float32)]
         + [jax.ShapeDtypeStruct((step, size), kind) for _, size, kind in pieces],
         in_specs=[
-            pl.BlockSpec((rows, tile), lambda j: (0, j + offset)),
-            whole(prev.shape),
-            whole(prev_t.shape),
-            whole(bias.shape),
-            whole(dots.shape),
-            whole(total.shape),
+            pl.BlockSpec((rows, tile), lambda j: (part, j + offset)),
+            tall(features),
+            pl.BlockSpec((features, rows), lambda j: (0, part)),
+            tall(1),
+            tall(1),
+            tall(features),
         ]
-        + tiles_of(tile, nexts),
-        out_specs=[whole(total.shape)]
+        + tiles_of(tile, nexts)
+        + [pl.BlockSpec((tile, features), lambda j: (j, 0)) for _ in carry],
+        out_specs=[whole(shape)]
         + [pl.BlockSpec((tile, size), lambda j: (j, 0)) for _, size, _ in pieces],
         scratch_shapes=[
             pltpu.VMEM((tile, features), jnp.bfloat16),
@@ -175,7 +185,7 @@
             bytes_accessed=2 * rows * step,
             transcendentals=rows * step,
         ),
-    )(grad, prev, prev_t, bias, dots, total, *[x for x, _ in nexts])
+    )(grad, prev, prev_t, bias, dots, total, *[x for x, _ in nexts], *carry)
 
 
 def body(parts, cols, grid_rows, grad_table, prev_embed, next_embed, log_norm):
@@ -240,6 +250,20 @@
         dots = lax.psum(dots, "col")
     dots = dots[:, None]
 
+    def block(sums, col):
+        code = jnp.bitwise_xor(col, r)
+        place = jnp.where(code == 1, 2, jnp.where(code == 2, 1, code))
+        return lax.dynamic_slice_in_dim(sums, place * share, share, 1)
+
+    def shares(sums):
+        return [block(sums, (c + a) % cols).astype(jnp.bfloat16) for a in range(1, cols)]
+
+    def collect(sums, away):
+        kept = block(sums, c)
+        for a in range(1, cols):
+            kept = kept + shift(away[a - 1], a).astype(jnp.float32)
+        return kept
+
     bias = bias - math.log2(scale)
     total = jnp.zeros((rows, features), jnp.float32)
     ends, sent = [], []
@@ -248,9 +272,16 @@
             total, sent[k - 2] = lax.optimization_barrier((total, sent[k - 2]))
         if paired and k >= 3:
             total, ends[k - 3] = lax.optimization_barrier((total, ends[k - 3]))
-        total, *sums = grad_terms(
-            grad_table, prev, prev_t, nxt, bias, dots, total, first, step, coef, pieces
-        )
+        common = (grad_table, prev, prev_t, nxt, bias, dots)
+        if paired and k == len(starts) - 1:
+            upper, carry = grad_terms(
+                *common, total, first, step, coef, ((0, features, jnp.float32),), (), 2, 0
+            )
+            total, upper_away = lax.optimization_barrier((total, shares(upper)))
+            upper_grad = collect(upper, upper_away)
+            total, *sums = grad_terms(*common, total, first, step, coef, pieces, (carry,), 2, 1)
+        else:
+            total, *sums = grad_terms(*common, total, first, step, coef, pieces)
         if paired:
             own, far, give = sums
             got = swap(give, 1)
@@ -261,21 +292,12 @@
         else:
             ends.append(lax.psum_scatter(sums[0], "row", scatter_dimension=1, tiled=True))
     if paired:
+        sent[-1], away = lax.optimization_barrier((sent[-1], shares(total)))
         ends[-1] = ends[-1] + swap(sent[-1], 2).astype(jnp.float32)
-    next_grad = jnp.concatenate(ends, axis=0)
-
-    if paired:
-        def block(col):
-            code = jnp.bitwise_xor(col, r)
-            place = jnp.where(code == 1, 2, jnp.where(code == 2, 1, code))
-            return lax.dynamic_slice_in_dim(total, place * share, share, 1)
-
-        prev_grad = block(c)
-        for a in range(1, cols):
-            away = block((c + a) % cols).astype(jnp.bfloat16)
-            prev_grad = prev_grad + shift(away, a).astype(jnp.float32)
+        prev_grad = jnp.concatenate([upper_grad, collect(total, away)], axis=0)
     else:
         prev_grad = lax.psum_scatter(total, "col", scatter_dimension=1, tiled=True)
+    next_grad = jnp.concatenate(ends, axis=0)
     return (prev_grad, next_grad)
 
 

time: 278 us -> 249 us (0.90)
  waiting for transfers between devices: 75.1 us -> 49.6 us
  starting transfers between devices: 41.8 us -> 34.1 us
  Pallas kernels: 131 us -> 136 us
    ppermute x9 -> x12, waiting for transfers between devices: 53 us -> 38.4 us  [shift(): return lax.ppermute(x, 'col', [(i, (i + by) % cols) for i in range(cols)])]
    ppermute x17, waiting for transfers between devices: 15.4 us -> 6.6 us  [swap(): return lax.ppermute(x, 'row', [(i, i ^ bit) for i in range(grid_rows)])]
    ppermute x17, starting transfers between devices: 24.1 us -> 18.4 us  [swap(): return lax.ppermute(x, 'row', [(i, i ^ bit) for i in range(grid_rows)])]
    pallas_call x4 -> x5, Pallas kernels: 89.8 us -> 93.5 us  [grad_terms(): pl.pallas_call(functools.partial(grads_kernel, coef, pieces, len(nexts),...]
    ppermute x9 -> x12, starting transfers between devices: 14.9 us -> 12.8 us  [shift(): return lax.ppermute(x, 'col', [(i, (i + by) % cols) for i in range(cols)])]
    unnamed x35 -> x39, local copies, waits for them, and re-layouts: 6.88 us -> 7.2 us
  transfers between devices with their start and end apart: 29 -> 32, of which waited for: 11 -> 13; matrix products, arithmetic and copies ran while one was open for 7% -> 7% of each run, Pallas kernels for 28% -> 43%
where the time goes in v3:
time: 249 us; the launch traced here: 248 us
  Pallas kernels  136 us (55%)
  waiting for transfers between devices  49.6 us (20%)
  starting transfers between devices  34.1 us (14%)
  local copies, waits for them, and re-layouts  19.4 us (8%)
  other arithmetic  8.32 us (3%)
    pallas_call x5, Pallas kernels, grad_terms(): pl.pallas_call(functools.partial(grads_kernel, coef, pieces, len(nexts),...  93.5 us
    ppermute x12, waiting for transfers between devices, shift(): return lax.ppermute(x, 'col', [(i, (i + by) % cols) for i in range(cols)])  38.4 us
    pallas_call x4, Pallas kernels, row_dots(): pl.pallas_call(functools.partial(dots_kernel, coef, len(nexts)), grid=(st...  35.3 us
    ppermute x17, starting transfers between devices, swap(): return lax.ppermute(x, 'row', [(i, i ^ bit) for i in range(grid_rows)])  18.4 us
    ppermute x12, starting transfers between devices, shift(): return lax.ppermute(x, 'col', [(i, (i + by) % cols) for i in range(cols)])  12.8 us
    unnamed x39, local copies, waits for them, and re-layouts  7.2 us
    pallas_call x1, Pallas kernels, arrange(): pl.pallas_call(arrange_kernel, grid_spec=pltpu.PrefetchScalarGridSpec(num...  6.9 us
    ppermute x17, waiting for transfers between devices, swap(): return lax.ppermute(x, 'row', [(i, i ^ bit) for i in range(grid_rows)])  6.6 us
  transfers between devices with their start and end apart: 32, of which 13 were waited for; matrix products, arithmetic and copies ran while one was open for 7% of the time, Pallas kernels for 43%

profile of v3, /device:TPU:9, one launch (start us, length us, event | category | flops | bytes accessed | tf_op | source)
XLA Modules:
  0.0 248.3 jit_solution(5781944995622841826)
XLA Ops:
  0.6 1.8 bitcast_dynamic-update-slice_fusion.7
  2.5 2.3 collective-permute-start.2
  6.2 2.7 %fusion = (bf16[2048,128]{1,0:T(8,128)(2,1)S(1)}, bf16[2048,128]{1,0:T(8,128)(2,1)}, bf16[2048,128]{1,0:T(8,128)(2,1)S(1)}, bf16[2048,128]{1,0:T(8,128)(2,1)}) fusion(bf16[8192,128]{1,0:T(8,128)(2,1)} %rest_0_.17), kind=kLoop, calls=%fused_computation.30 | loop fusion | bytes 4194304 | tf_op jit(solution)/shard_map/slice | solution.py:220
  10.3 11.0 %collective-permute-done = bf16[1024,128]{1,0:T(8,128)(2,1)S(1)} collective-permute-done((bf16[1024,128]{1,0:T(8,128)(2,1)}, bf16[1024,128]{1,0:T(8,128)(2,1)S(1)}, u32[]{:S(2)}, u32[]{:S(2)}) %collective-permute-start) | collective-permute-done | bytes 262176 | tf_op jit(solution)/shard_map/ppermute | solution.py:206
  24.8 3.2 %collective-permute-done.1 = bf16[1024,128]{1,0:T(8,128)(2,1)S(1)} collective-permute-done((bf16[1024,128]{1,0:T(8,128)(2,1)S(1)}, bf16[1024,128]{1,0:T(8,128)(2,1)S(1)}, u32[]{:S(2)}, u32[]{:S(2)}) %collective-permute-start.1) | collective-permute-done | bytes 262176 | tf_op jit(solution)/shard_map/ppermute | solution.py:209
  35.0 1.7 collective-permute-start.8
  39.5 2.9 %collective-permute-start.10 = (bf16[2048,128]{1,0:T(8,128)(2,1)S(1)}, bf16[2048,128]{1,0:T(8,128)(2,1)}, u32[]{:S(2)}, u32[]{:S(2)}) collective-permute-start(bf16[2048,128]{1,0:T(8,128)(2,1)S(1)} %collective-permute-done.9.rest_1_), channel_id=1, source_target_pairs={{0,1},{1,0},{2,3},{3,2},{4,5},{5,4},{6,7},{7,6},{8,9},{9,8},{10,11... | collective-permute-start | bytes 1572872 | tf_op jit(solution)/shard_map/ppermute | solution.py:203
  43.2 6.9 %shard_map.59 = (bf16[2048,512]{1,0:T(8,128)(2,1)}, bf16[512,2048]{1,0:T(8,128)(2,1)}) custom-call(s32[6]{0:T(128)} %stack.54.places_ref, bf16[4,2,1024,128]{3,2,1,0:T(8,128)(2,1)} %bitcast.14.arrived_ref), custom_call_target="tpu_custom_call" | custom-call | bytes 6291456 | tf_op jit(solution)/shard_map/pallas_call | solution.py:27
  50.1 3.4 %collective-permute-done.11.rest_1_ = bf16[2048,128]{1,0:T(8,128)(2,1)S(1)} collective-permute-done((bf16[2048,128]{1,0:T(8,128)(2,1)}, bf16[2048,128]{1,0:T(8,128)(2,1)S(1)}, u32[]{:S(2)}, u32[]{:S(2)}) %collective-permute-start.11) | collective-permute-done | bytes 524320 | tf_op jit(solution)/shard_map/ppermute | solution.py:203
  53.6 3.3 %collective-permute-start.12 = (bf16[2048,128]{1,0:T(8,128)(2,1)S(1)}, bf16[2048,128]{1,0:T(8,128)(2,1)S(1)}, u32[]{:S(2)}, u32[]{:S(2)}) collective-permute-start(bf16[2048,128]{1,0:T(8,128)(2,1)S(1)} %collective-permute-done.11.rest_1_), channel_id=1, source_target_pairs={{0,1},{1,0},{2,3},{3,2},{4,5},{5,4},{6,7},{7,6},{8,9},{9,8},{10,11... | collective-permute-start | bytes 1572872 | tf_op jit(solution)/shard_map/ppermute | solution.py:203
  57.0 8.7 %shard_map.60.total_ref = f32[2048,128]{1,0:T(8,128)S(1)} custom-call(bf16[2048,8192]{1,0:T(8,128)(2,1)} %grad_ref.17, bf16[2048,512]{1,0:T(8,128)(2,1)} %get-tuple-element.34.prev_ref, f32[2048,1]{1,0:T(8,128)S(1)} %copy.9.bias_ref, f32[2048,128]{1,0:T(8,128)S(1)} %broadcast_in_dim.7.total_ref, bf16[8192,128]{1,0:T(8,128)(2,1)} %rest_0_.17, ...), custom_call_target="tpu_custom_call" | custom-call | flops 4294967296 | bytes 8388608 | tf_op jit(solution)/shard_map/pallas_call | solution.py:129
  65.7 9.2 %shard_map.61.total_ref = f32[2048,128]{1,0:T(8,128)S(1)} custom-call(bf16[2048,8192]{1,0:T(8,128)(2,1)} %grad_ref.17, bf16[2048,512]{1,0:T(8,128)(2,1)} %get-tuple-element.34.prev_ref, f32[2048,1]{1,0:T(8,128)S(1)} %copy.9.bias_ref, f32[2048,128]{1,0:T(8,128)S(1)} %shard_map.60.total_ref, bf16[8192,128]{1,0:T(8,128)(2,1)} %rest_0_.17, ...), custom_call_target="tpu_custom_call" | custom-call | flops 4294967296 | bytes 8388608 | tf_op jit(solution)/shard_map/pallas_call | solution.py:129
  74.9 8.7 %shard_map.62.total_ref = f32[2048,128]{1,0:T(8,128)S(1)} custom-call(bf16[2048,8192]{1,0:T(8,128)(2,1)} %grad_ref.17, bf16[2048,512]{1,0:T(8,128)(2,1)} %get-tuple-element.34.prev_ref, f32[2048,1]{1,0:T(8,128)S(1)} %copy.9.bias_ref, f32[2048,128]{1,0:T(8,128)S(1)} %shard_map.61.total_ref, bf16[8192,128]{1,0:T(8,128)(2,1)} %rest_0_.17, ...), custom_call_target="tpu_custom_call" | custom-call | flops 4294967296 | bytes 8388608 | tf_op jit(solution)/shard_map/pallas_call | solution.py:129
  83.7 8.7 %shard_map.63 = f32[2048,128]{1,0:T(8,128)S(1)} custom-call(bf16[2048,8192]{1,0:T(8,128)(2,1)} %grad_ref.17, bf16[2048,512]{1,0:T(8,128)(2,1)} %get-tuple-element.34.prev_ref, f32[2048,1]{1,0:T(8,128)S(1)} %copy.9.bias_ref, f32[2048,128]{1,0:T(8,128)S(1)} %shard_map.62.total_ref, bf16[8192,128]{1,0:T(8,128)(2,1)} %rest_0_.17, ...), custom_call_target="tpu_custom_call" | custom-call | flops 4294967296 | bytes 8388608 | tf_op jit(solution)/shard_map/pallas_call | solution.py:129
  92.7 1.6 collective-permute-start.17
  95.2 1.5 collective-permute-start.15
  99.5 2.5 %broadcast_in_dim.8.total_ref = f32[2048,512]{1,0:T(8,128)} broadcast(f32[]{:T(128)} %constant.76.clone.1), dimensions={} | broadcast | bytes 4194308 | tf_op jit(solution)/shard_map/broadcast_in_dim | solution.py:268
  102.0 21.5 %shard_map.64 = (f32[2048,512]{1,0:T(8,128)}, f32[2048,128]{1,0:T(8,128)}, f32[2048,128]{1,0:T(8,128)}, bf16[2048,256]{1,0:T(8,128)(2,1)}) custom-call(bf16[2048,8192]{1,0:T(8,128)(2,1)} %grad_ref.17, bf16[2048,512]{1,0:T(8,128)(2,1)} %get-tuple-element.34.prev_ref, bf16[512,2048]{1,0:T(8,128)(2,1)} %get-tuple-element.35.prev_t_ref, ...), custom_call_target="tpu_custom_call" | custom-call | flops 12884901888 | bytes 8388608 | tf_op jit(solution)/shard_map/pallas_call | solution.py:161
  124.9 22.8 %shard_map.65 = (f32[2048,512]{1,0:T(8,128)}, f32[2048,128]{1,0:T(8,128)}, f32[2048,128]{1,0:T(8,128)}, bf16[2048,256]{1,0:T(8,128)(2,1)}) custom-call(bf16[2048,8192]{1,0:T(8,128)(2,1)} %grad_ref.17, bf16[2048,512]{1,0:T(8,128)(2,1)} %get-tuple-element.34.prev_ref, bf16[512,2048]{1,0:T(8,128)(2,1)} %get-tuple-element.35.prev_t_ref, ...), custom_call_target="tpu_custom_call" | custom-call | flops 12884901888 | bytes 8388608 | tf_op jit(solution)/shard_map/pallas_call | solution.py:161
  152.1 22.7 %shard_map.66 = (f32[2048,512]{1,0:T(8,128)}, f32[2048,128]{1,0:T(8,128)}, f32[2048,128]{1,0:T(8,128)}, bf16[2048,256]{1,0:T(8,128)(2,1)}) custom-call(bf16[2048,8192]{1,0:T(8,128)(2,1)} %grad_ref.17, bf16[2048,512]{1,0:T(8,128)(2,1)} %get-tuple-element.34.prev_ref, bf16[512,2048]{1,0:T(8,128)(2,1)} %get-tuple-element.35.prev_t_ref, ...), custom_call_target="tpu_custom_call" | custom-call | flops 12884901888 | bytes 8388608 | tf_op jit(solution)/shard_map/pallas_call | solution.py:161
  176.4 13.3 %shard_map.67 = (f32[1024,512]{1,0:T(8,128)}, f32[2048,512]{1,0:T(8,128)}) custom-call(bf16[2048,8192]{1,0:T(8,128)(2,1)} %grad_ref.17, bf16[2048,512]{1,0:T(8,128)(2,1)} %get-tuple-element.34.prev_ref, bf16[512,2048]{1,0:T(8,128)(2,1)} %get-tuple-element.35.prev_t_ref, f32[2048,1]{1,0:T(8,128)} %copy.16.bias_ref, f32[2048,1]{1,0:T(8,128)} %copy.17.dot_ref, ...), custom_call_target="tpu_custom_call" | custom-call | flops 6442450944 | bytes 4194304 | tf_op jit(solution)/shard_map/pallas_call | solution.py:161
  189.6 2.3 dynamic-slice_convert_fusion.3
  192.0 1.5 collective-permute-start.21
  193.5 2.5 %collective-permute-start.22 = (bf16[1024,128]{1,0:T(8,128)(2,1)}, bf16[1024,128]{1,0:T(8,128)(2,1)}, u32[]{:S(2)}, u32[]{:S(2)}) collective-permute-start(bf16[1024,128]{1,0:T(8,128)(2,1)} %get-tuple-element.49), channel_id=1, source_target_pairs={{0,8},{4,12},{8,0},{12,4},{1,9},{5,13},{9,1},{13,5},{2,10},{6,14},... | collective-permute-start | bytes 786440 | tf_op jit(solution)/shard_map/ppermute | solution.py:206
  196.0 13.3 %shard_map.68 = (f32[1024,512]{1,0:T(8,128)}, f32[2048,128]{1,0:T(8,128)}, f32[2048,128]{1,0:T(8,128)}, bf16[2048,256]{1,0:T(8,128)(2,1)}) custom-call(bf16[2048,8192]{1,0:T(8,128)(2,1)} %grad_ref.17, bf16[2048,512]{1,0:T(8,128)(2,1)} %get-tuple-element.34.prev_ref, bf16[512,2048]{1,0:T(8,128)(2,1)} %get-tuple-element.35.prev_t_ref, ...), custom_call_target="tpu_custom_call" | custom-call | flops 6442450944 | bytes 4194304 | tf_op jit(solution)/shard_map/pallas_call | solution.py:161
  212.1 4.3 %collective-permute-done.22 = bf16[1024,128]{1,0:T(8,128)(2,1)} collective-permute-done((bf16[1024,128]{1,0:T(8,128)(2,1)}, bf16[1024,128]{1,0:T(8,128)(2,1)}, u32[]{:S(2)}, u32[]{:S(2)}) %collective-permute-start.22) | collective-permute-done | bytes 262176 | tf_op jit(solution)/shard_map/ppermute | solution.py:206
  216.3 2.4 collective-permute-done.23
  223.0 1.7 collective-permute-done.30
  224.9 2.4 collective-permute-done.25
  227.3 15.0 %collective-permute-done.26 = bf16[1024,128]{1,0:T(8,128)(2,1)S(1)} collective-permute-done((bf16[1024,128]{1,0:T(8,128)(2,1)S(1)}, bf16[1024,128]{1,0:T(8,128)(2,1)S(1)}, u32[]{:S(2)}, u32[]{:S(2)}) %collective-permute-start.26) | collective-permute-done | bytes 262176 | tf_op jit(solution)/shard_map/ppermute | solution.py:206
  242.2 2.4 collective-permute-done.27
  246.0 2.3 pad_maximum_fusion
  (106 shorter events, 36.7 us)
Async XLA Ops:
  2.5 22.3 %collective-permute-start.2 = (bf16[1024,128]{1,0:T(8,128)(2,1)}, bf16[1024,128]{1,0:T(8,128)(2,1)S(1)}, u32[]{:S(2)}, u32[]{:S(2)}) collective-permute-start(bf16[1024,128]{1,0:T(8,128)(2,1)} %get-tuple-element.67), channel_id=1, source_target_pairs={{0,8},{4,12},{8,0},{12,4},{1,9},{5,13},{9,1},{13,5},{2,10},{6,14},... | collective-permute-start | bytes 786440 | tf_op jit(solution)/shard_map/ppermute | solution.py:206
  4.8 16.5 %collective-permute-start = (bf16[1024,128]{1,0:T(8,128)(2,1)}, bf16[1024,128]{1,0:T(8,128)(2,1)S(1)}, u32[]{:S(2)}, u32[]{:S(2)}) collective-permute-start(bf16[1024,128]{1,0:T(8,128)(2,1)} %get-tuple-element.67), channel_id=1, source_target_pairs={{0,12},{4,0},{8,4},{12,8},{1,13},{5,1},{9,5},{13,9},{2,14},{6,2},{... | collective-permute-start | bytes 786440 | tf_op jit(solution)/shard_map/ppermute | solution.py:206
  4.9 51.9 %collective-permute-start.7 = (bf16[8192,128]{1,0:T(8,128)(2,1)}, bf16[8192,128]{1,0:T(8,128)(2,1)}, u32[]{:S(2)}, u32[]{:S(2)}) collective-permute-start(bf16[8192,128]{1,0:T(8,128)(2,1)} %rest_0_.17), channel_id=1, source_target_pairs={{0,1},{1,0},{2,3},{3,2},{4,5},{5,4},{6,7},{7,6},{8,9},{9,8},{10,11... | collective-permute-start | bytes 6291464 | tf_op jit(solution)/shard_map/ppermute | solution.py:203
  8.8 23.5 %collective-permute-start.9 = (bf16[2048,128]{1,0:T(8,128)(2,1)S(1)}, bf16[2048,128]{1,0:T(8,128)(2,1)S(1)}, u32[]{:S(2)}, u32[]{:S(2)}) collective-permute-start(bf16[2048,128]{1,0:T(8,128)(2,1)S(1)} %get-tuple-element.76), channel_id=1, source_target_pairs={{0,2},{1,3},{2,0},{3,1},{4,6},{5,7},{6,4},{7,5},{8,10},{9,11},{10,... | collective-permute-start | bytes 1572872 | tf_op jit(solution)/shard_map/ppermute | solution.py:203
  10.0 23.7 %collective-permute-start.6 = (bf16[2048,128]{1,0:T(8,128)(2,1)}, bf16[2048,128]{1,0:T(8,128)(2,1)}, u32[]{:S(2)}, u32[]{:S(2)}) collective-permute-start(bf16[2048,128]{1,0:T(8,128)(2,1)} %get-tuple-element.77), channel_id=1, source_target_pairs={{0,2},{1,3},{2,0},{3,1},{4,6},{5,7},{6,4},{7,5},{8,10},{9,11},{10,... | collective-permute-start | bytes 1572872 | tf_op jit(solution)/shard_map/ppermute | solution.py:203
  21.3 6.7 %collective-permute-start.1 = (bf16[1024,128]{1,0:T(8,128)(2,1)S(1)}, bf16[1024,128]{1,0:T(8,128)(2,1)S(1)}, u32[]{:S(2)}, u32[]{:S(2)}) collective-permute-start(bf16[1024,128]{1,0:T(8,128)(2,1)S(1)} %collective-permute-done), channel_id=1, source_target_pairs={{0,16},{16,0},{1,17},{17,1},{2,18},{18,2},{3,19},{19,3},{4,20},{20... | collective-permute-start | bytes 786440 | tf_op jit(solution)/shard_map/ppermute | solution.py:209
  24.8 6.3 %collective-permute-start.4 = (bf16[1024,128]{1,0:T(8,128)(2,1)}, bf16[1024,128]{1,0:T(8,128)(2,1)S(1)}, u32[]{:S(2)}, u32[]{:S(2)}) collective-permute-start(bf16[1024,128]{1,0:T(8,128)(2,1)} %get-tuple-element.67), channel_id=1, source_target_pairs={{0,4},{4,8},{8,12},{12,0},{1,5},{5,9},{9,13},{13,1},{2,6},{6,10},{... | collective-permute-start | bytes 786440 | tf_op jit(solution)/shard_map/ppermute | solution.py:206
  27.9 7.0 %collective-permute-start.3 = (bf16[1024,128]{1,0:T(8,128)(2,1)S(1)}, bf16[1024,128]{1,0:T(8,128)(2,1)S(1)}, u32[]{:S(2)}, u32[]{:S(2)}) collective-permute-start(bf16[1024,128]{1,0:T(8,128)(2,1)S(1)} %collective-permute-done.2), channel_id=1, source_target_pairs={{0,16},{16,0},{1,17},{17,1},{2,18},{18,2},{3,19},{19,3},{4,20},{20... | collective-permute-start | bytes 786440 | tf_op jit(solution)/shard_map/ppermute | solution.py:209
  31.1 19.0 %collective-permute-start.13 = (bf16[2048,128]{1,0:T(8,128)(2,1)S(1)}, bf16[2048,128]{1,0:T(8,128)(2,1)S(1)}, u32[]{:S(2)}, u32[]{:S(2)}) collective-permute-start(bf16[2048,128]{1,0:T(8,128)(2,1)S(1)} %get-tuple-element.74), channel_id=1, source_target_pairs={{0,2},{1,3},{2,0},{3,1},{4,6},{5,7},{6,4},{7,5},{8,10},{9,11},{10,... | collective-permute-start | bytes 1572872 | tf_op jit(solution)/shard_map/ppermute | solution.py:203
  32.3 21.3 %collective-permute-start.11 = (bf16[2048,128]{1,0:T(8,128)(2,1)}, bf16[2048,128]{1,0:T(8,128)(2,1)S(1)}, u32[]{:S(2)}, u32[]{:S(2)}) collective-permute-start(bf16[2048,128]{1,0:T(8,128)(2,1)} %get-tuple-element.75), channel_id=1, source_target_pairs={{0,2},{1,3},{2,0},{3,1},{4,6},{5,7},{6,4},{7,5},{8,10},{9,11},{10,... | collective-permute-start | bytes 1572872 | tf_op jit(solution)/shard_map/ppermute | solution.py:203
  33.7 5.8 %collective-permute-start.5 = (bf16[1024,128]{1,0:T(8,128)(2,1)S(1)}, bf16[1024,128]{1,0:T(8,128)(2,1)S(1)}, u32[]{:S(2)}, u32[]{:S(2)}) collective-permute-start(bf16[1024,128]{1,0:T(8,128)(2,1)S(1)} %collective-permute-done.4), channel_id=1, source_target_pairs={{0,16},{16,0},{1,17},{17,1},{2,18},{18,2},{3,19},{19,3},{4,20},{20... | collective-permute-start | bytes 786440 | tf_op jit(solution)/shard_map/ppermute | solution.py:209
  35.0 21.9 %collective-permute-start.8 = (bf16[2048,128]{1,0:T(8,128)(2,1)}, bf16[2048,128]{1,0:T(8,128)(2,1)}, u32[]{:S(2)}, u32[]{:S(2)}) collective-permute-start(bf16[2048,128]{1,0:T(8,128)(2,1)} %collective-permute-done.6.rest_1_), channel_id=1, source_target_pairs={{0,1},{1,0},{2,3},{3,2},{4,5},{5,4},{6,7},{7,6},{8,9},{9,8},{10,11... | collective-permute-start | bytes 1572872 | tf_op jit(solution)/shard_map/ppermute | solution.py:203
  39.5 26.2 %collective-permute-start.10 = (bf16[2048,128]{1,0:T(8,128)(2,1)S(1)}, bf16[2048,128]{1,0:T(8,128)(2,1)}, u32[]{:S(2)}, u32[]{:S(2)}) collective-permute-start(bf16[2048,128]{1,0:T(8,128)(2,1)S(1)} %collective-permute-done.9.rest_1_), channel_id=1, source_target_pairs={{0,1},{1,0},{2,3},{3,2},{4,5},{5,4},{6,7},{7,6},{8,9},{9,8},{10,11... | collective-permute-start | bytes 1572872 | tf_op jit(solution)/shard_map/ppermute | solution.py:203
  50.1 33.6 %collective-permute-start.14 = (bf16[2048,128]{1,0:T(8,128)(2,1)S(1)}, bf16[2048,128]{1,0:T(8,128)(2,1)S(1)}, u32[]{:S(2)}, u32[]{:S(2)}) collective-permute-start(bf16[2048,128]{1,0:T(8,128)(2,1)S(1)} %collective-permute-done.13.rest_1_), channel_id=1, source_target_pairs={{0,1},{1,0},{2,3},{3,2},{4,5},{5,4},{6,7},{7,6},{8,9},{9,8},{10,11... | collective-permute-start | bytes 1572872 | tf_op jit(solution)/shard_map/ppermute | solution.py:203
  53.6 21.4 %collective-permute-start.12 = (bf16[2048,128]{1,0:T(8,128)(2,1)S(1)}, bf16[2048,128]{1,0:T(8,128)(2,1)S(1)}, u32[]{:S(2)}, u32[]{:S(2)}) collective-permute-start(bf16[2048,128]{1,0:T(8,128)(2,1)S(1)} %collective-permute-done.11.rest_1_), channel_id=1, source_target_pairs={{0,1},{1,0},{2,3},{3,2},{4,5},{5,4},{6,7},{7,6},{8,9},{9,8},{10,11... | collective-permute-start | bytes 1572872 | tf_op jit(solution)/shard_map/ppermute | solution.py:203
  92.7 5.4 %collective-permute-start.17 = (f32[16,128]{1,0:T(8,128)S(1)}, f32[16,128]{1,0:T(8,128)S(1)}, u32[]{:S(2)}, u32[]{:S(2)}) collective-permute-start(f32[16,128]{1,0:T(8,128)S(1)} %bitcast.30), channel_id=1, source_target_pairs={{0,12},{4,0},{8,4},{12,8},{1,13},{5,1},{9,5},{13,9},{2,14},{6,2},{... | collective-permute-start | bytes 24584 | tf_op jit(solution)/shard_map/ppermute | solution.py:206
  94.3 3.8 %collective-permute-start.16 = (f32[16,128]{1,0:T(8,128)S(1)}, f32[16,128]{1,0:T(8,128)S(1)}, u32[]{:S(2)}, u32[]{:S(2)}) collective-permute-start(f32[16,128]{1,0:T(8,128)S(1)} %bitcast.31), channel_id=1, source_target_pairs={{0,8},{4,12},{8,0},{12,4},{1,9},{5,13},{9,1},{13,5},{2,10},{6,14},... | collective-permute-start | bytes 24584 | tf_op jit(solution)/shard_map/ppermute | solution.py:206
  95.2 2.9 %collective-permute-start.15 = (f32[16,128]{1,0:T(8,128)S(1)}, f32[16,128]{1,0:T(8,128)S(1)}, u32[]{:S(2)}, u32[]{:S(2)}) collective-permute-start(f32[16,128]{1,0:T(8,128)S(1)} %bitcast.32), channel_id=1, source_target_pairs={{0,4},{4,8},{8,12},{12,0},{1,5},{5,9},{9,13},{13,1},{2,6},{6,10},{... | collective-permute-start | bytes 24584 | tf_op jit(solution)/shard_map/ppermute | solution.py:206
  123.5 24.4 %collective-permute-start.18 = (bf16[2048,256]{1,0:T(8,128)(2,1)}, bf16[2048,256]{1,0:T(8,128)(2,1)}, u32[]{:S(2)}, u32[]{:S(2)}) collective-permute-start(bf16[2048,256]{1,0:T(8,128)(2,1)} %get-tuple-element.39), channel_id=1, source_target_pairs={{0,1},{1,0},{2,3},{3,2},{4,5},{5,4},{6,7},{7,6},{8,9},{9,8},{10,11... | collective-permute-start | bytes 3145736 | tf_op jit(solution)/shard_map/ppermute | solution.py:203
  147.7 2.9 %collective-permute-start.19 = (bf16[2048,256]{1,0:T(8,128)(2,1)}, bf16[2048,256]{1,0:T(8,128)(2,1)S(1)}, u32[]{:S(2)}, u32[]{:S(2)}) collective-permute-start(bf16[2048,256]{1,0:T(8,128)(2,1)} %get-tuple-element.43), channel_id=1, source_target_pairs={{0,1},{1,0},{2,3},{3,2},{4,5},{5,4},{6,7},{7,6},{8,9},{9,8},{10,11... | collective-permute-start | bytes 3145736 | tf_op jit(solution)/shard_map/ppermute | solution.py:203
  149.1 26.0 %collective-permute-start.20 = (bf16[2048,128]{1,0:T(8,128)(2,1)S(1)}, bf16[2048,128]{1,0:T(8,128)(2,1)S(1)}, u32[]{:S(2)}, u32[]{:S(2)}) collective-permute-start(bf16[2048,128]{1,0:T(8,128)(2,1)S(1)} %add_convert_fusion.3), channel_id=1, source_target_pairs={{0,2},{1,3},{2,0},{3,1},{4,6},{5,7},{6,4},{7,5},{8,10},{9,11},{10,... | collective-permute-start | bytes 1572872 | tf_op jit(solution)/shard_map/ppermute | solution.py:203
  150.8 58.6 %collective-permute-start.28 = (bf16[2048,128]{1,0:T(8,128)(2,1)S(1)}, bf16[2048,128]{1,0:T(8,128)(2,1)S(1)}, u32[]{:S(2)}, u32[]{:S(2)}) collective-permute-start(bf16[2048,128]{1,0:T(8,128)(2,1)S(1)} %add_convert_fusion.2), channel_id=1, source_target_pairs={{0,2},{1,3},{2,0},{3,1},{4,6},{5,7},{6,4},{7,5},{8,10},{9,11},{10,... | collective-permute-start | bytes 1572872 | tf_op jit(solution)/shard_map/ppermute | solution.py:203
  174.7 36.4 %collective-permute-start.29 = (bf16[2048,256]{1,0:T(8,128)(2,1)}, bf16[2048,256]{1,0:T(8,128)(2,1)S(1)}, u32[]{:S(2)}, u32[]{:S(2)}) collective-permute-start(bf16[2048,256]{1,0:T(8,128)(2,1)} %get-tuple-element.62), channel_id=1, source_target_pairs={{0,1},{1,0},{2,3},{3,2},{4,5},{5,4},{6,7},{7,6},{8,9},{9,8},{10,11... | collective-permute-start | bytes 3145736 | tf_op jit(solution)/shard_map/ppermute | solution.py:203
  192.0 20.1 %collective-permute-start.21 = (bf16[1024,128]{1,0:T(8,128)(2,1)}, bf16[1024,128]{1,0:T(8,128)(2,1)}, u32[]{:S(2)}, u32[]{:S(2)}) collective-permute-start(bf16[1024,128]{1,0:T(8,128)(2,1)} %get-tuple-element.48), channel_id=1, source_target_pairs={{0,4},{4,8},{8,12},{12,0},{1,5},{5,9},{9,13},{13,1},{2,6},{6,10},{... | collective-permute-start | bytes 786440 | tf_op jit(solution)/shard_map/ppermute | solution.py:206
  193.5 22.8 %collective-permute-start.22 = (bf16[1024,128]{1,0:T(8,128)(2,1)}, bf16[1024,128]{1,0:T(8,128)(2,1)}, u32[]{:S(2)}, u32[]{:S(2)}) collective-permute-start(bf16[1024,128]{1,0:T(8,128)(2,1)} %get-tuple-element.49), channel_id=1, source_target_pairs={{0,8},{4,12},{8,0},{12,4},{1,9},{5,13},{9,1},{13,5},{2,10},{6,14},... | collective-permute-start | bytes 786440 | tf_op jit(solution)/shard_map/ppermute | solution.py:206
  196.0 22.7 %collective-permute-start.23 = (bf16[1024,128]{1,0:T(8,128)(2,1)S(1)}, bf16[1024,128]{1,0:T(8,128)(2,1)}, u32[]{:S(2)}, u32[]{:S(2)}) collective-permute-start(bf16[1024,128]{1,0:T(8,128)(2,1)S(1)} %get-tuple-element.50), channel_id=1, source_target_pairs={{0,12},{4,0},{8,4},{12,8},{1,13},{5,1},{9,5},{13,9},{2,14},{6,2},{... | collective-permute-start | bytes 786440 | tf_op jit(solution)/shard_map/ppermute | solution.py:206
  209.3 10.8 %collective-permute-start.24 = (bf16[2048,256]{1,0:T(8,128)(2,1)}, bf16[2048,256]{1,0:T(8,128)(2,1)S(1)}, u32[]{:S(2)}, u32[]{:S(2)}) collective-permute-start(bf16[2048,256]{1,0:T(8,128)(2,1)} %get-tuple-element.55), channel_id=1, source_target_pairs={{0,1},{1,0},{2,3},{3,2},{4,5},{5,4},{6,7},{7,6},{8,9},{9,8},{10,11... | collective-permute-start | bytes 3145736 | tf_op jit(solution)/shard_map/ppermute | solution.py:203
  211.6 13.2 %collective-permute-start.30 = (bf16[2048,128]{1,0:T(8,128)(2,1)S(1)}, bf16[2048,128]{1,0:T(8,128)(2,1)S(1)}, u32[]{:S(2)}, u32[]{:S(2)}) collective-permute-start(bf16[2048,128]{1,0:T(8,128)(2,1)S(1)} %add_convert_fusion), channel_id=1, source_target_pairs={{0,2},{1,3},{2,0},{3,1},{4,6},{5,7},{6,4},{7,5},{8,10},{9,11},{10,... | collective-permute-start | bytes 1572872 | tf_op jit(solution)/shard_map/ppermute | solution.py:203
  220.3 7.0 %collective-permute-start.25 = (bf16[1024,128]{1,0:T(8,128)(2,1)S(1)}, bf16[1024,128]{1,0:T(8,128)(2,1)S(1)}, u32[]{:S(2)}, u32[]{:S(2)}) collective-permute-start(bf16[1024,128]{1,0:T(8,128)(2,1)S(1)} %get-tuple-element.56), channel_id=1, source_target_pairs={{0,4},{4,8},{8,12},{12,0},{1,5},{5,9},{9,13},{13,1},{2,6},{6,10},{... | collective-permute-start | bytes 786440 | tf_op jit(solution)/shard_map/ppermute | solution.py:206
  220.3 21.9 %collective-permute-start.26 = (bf16[1024,128]{1,0:T(8,128)(2,1)S(1)}, bf16[1024,128]{1,0:T(8,128)(2,1)S(1)}, u32[]{:S(2)}, u32[]{:S(2)}) collective-permute-start(bf16[1024,128]{1,0:T(8,128)(2,1)S(1)} %get-tuple-element.57), channel_id=1, source_target_pairs={{0,8},{4,12},{8,0},{12,4},{1,9},{5,13},{9,1},{13,5},{2,10},{6,14},... | collective-permute-start | bytes 786440 | tf_op jit(solution)/shard_map/ppermute | solution.py:206
  221.1 23.6 %collective-permute-start.27 = (bf16[1024,128]{1,0:T(8,128)(2,1)S(1)}, bf16[1024,128]{1,0:T(8,128)(2,1)S(1)}, u32[]{:S(2)}, u32[]{:S(2)}) collective-permute-start(bf16[1024,128]{1,0:T(8,128)(2,1)S(1)} %get-tuple-element.58), channel_id=1, source_target_pairs={{0,12},{4,0},{8,4},{12,8},{1,13},{5,1},{9,5},{13,9},{2,14},{6,2},{... | collective-permute-start | bytes 786440 | tf_op jit(solution)/shard_map/ppermute | solution.py:206
  222.5 23.3 %collective-permute-start.31 = (bf16[2048,128]{1,0:T(8,128)(2,1)S(1)}, bf16[2048,128]{1,0:T(8,128)(2,1)S(1)}, u32[]{:S(2)}, u32[]{:S(2)}) collective-permute-start(bf16[2048,128]{1,0:T(8,128)(2,1)S(1)} %add_convert_fusion.1), channel_id=1, source_target_pairs={{0,2},{1,3},{2,0},{3,1},{4,6},{5,7},{6,4},{7,5},{8,10},{9,11},{10,... | collective-permute-start | bytes 1572872 | tf_op jit(solution)/shard_map/ppermute | solution.py:203
  (16 other events, 243.9 us)

commit v4 on v3

--- a/solution.py
+++ b/solution.py
@@ -10,7 +10,7 @@
 
 LOG2E = math.log2(math.e)
 TILE = 512
-ROW_BLOCK = 512
+ROW_BLOCK = 256
 CHUNKS = 4
 NT = (((1,), (1,)), ((), ()))
 

time: 249 us -> 257 us (1.032)
  Pallas kernels: 136 us -> 145 us
    pallas_call x5, Pallas kernels: 93.5 us -> 103 us  [grad_terms(): pl.pallas_call(functools.partial(grads_kernel, coef, pieces, len(nexts),...]
  transfers between devices with their start and end apart: 32 -> 32, of which waited for: 13 -> 13; matrix products, arithmetic and copies ran while one was open for 7% -> 7% of each run, Pallas kernels for 43% -> 44%
where the time goes in v4:
time: 257 us
  Pallas kernels  145 us (56%)
  waiting for transfers between devices  48.5 us (19%)
  starting transfers between devices  34.2 us (13%)
  local copies, waits for them, and re-layouts  19.4 us (8%)
  other arithmetic  8.32 us (3%)
    pallas_call x5, Pallas kernels, grad_terms(): pl.pallas_call(functools.partial(grads_kernel, coef, pieces, len(nexts),...  103 us
    ppermute x12, waiting for transfers between devices, shift(): return lax.ppermute(x, 'col', [(i, (i + by) % cols) for i in range(cols)])  36.1 us
    pallas_call x4, Pallas kernels, row_dots(): pl.pallas_call(functools.partial(dots_kernel, coef, len(nexts)), grid=(st...  35.3 us
    ppermute x17, starting transfers between devices, swap(): return lax.ppermute(x, 'row', [(i, i ^ bit) for i in range(grid_rows)])  18.4 us
    ppermute x12, starting transfers between devices, shift(): return lax.ppermute(x, 'col', [(i, (i + by) % cols) for i in range(cols)])  12.9 us
    ppermute x17, waiting for transfers between devices, swap(): return lax.ppermute(x, 'row', [(i, i ^ bit) for i in range(grid_rows)])  7.8 us
    unnamed x39, local copies, waits for them, and re-layouts  7.2 us
    pallas_call x1, Pallas kernels, arrange(): pl.pallas_call(arrange_kernel, grid_spec=pltpu.PrefetchScalarGridSpec(num...  6.9 us
  transfers between devices with their start and end apart: 32, of which 13 were waited for; matrix products, arithmetic and copies ran while one was open for 7% of the time, Pallas kernels for 44%

profile of v4, /device:TPU:9, one launch (start us, length us, event | category | flops | bytes accessed | tf_op | source)
XLA Modules:
  0.0 256.5 jit_solution(17807521322853426339)
XLA Ops:
  0.6 1.8 bitcast_dynamic-update-slice_fusion.7
  2.5 2.3 collective-permute-start.2
  6.2 2.7 %fusion = (bf16[2048,128]{1,0:T(8,128)(2,1)S(1)}, bf16[2048,128]{1,0:T(8,128)(2,1)}, bf16[2048,128]{1,0:T(8,128)(2,1)S(1)}, bf16[2048,128]{1,0:T(8,128)(2,1)}) fusion(bf16[8192,128]{1,0:T(8,128)(2,1)} %rest_0_.17), kind=kLoop, calls=%fused_computation.30 | loop fusion | bytes 4194304 | tf_op jit(solution)/shard_map/slice | solution.py:220
  10.3 11.0 %collective-permute-done = bf16[1024,128]{1,0:T(8,128)(2,1)S(1)} collective-permute-done((bf16[1024,128]{1,0:T(8,128)(2,1)}, bf16[1024,128]{1,0:T(8,128)(2,1)S(1)}, u32[]{:S(2)}, u32[]{:S(2)}) %collective-permute-start) | collective-permute-done | bytes 262176 | tf_op jit(solution)/shard_map/ppermute | solution.py:206
  24.8 3.2 %collective-permute-done.1 = bf16[1024,128]{1,0:T(8,128)(2,1)S(1)} collective-permute-done((bf16[1024,128]{1,0:T(8,128)(2,1)S(1)}, bf16[1024,128]{1,0:T(8,128)(2,1)S(1)}, u32[]{:S(2)}, u32[]{:S(2)}) %collective-permute-start.1) | collective-permute-done | bytes 262176 | tf_op jit(solution)/shard_map/ppermute | solution.py:209
  35.0 1.7 collective-permute-start.8
  39.5 2.9 %collective-permute-start.10 = (bf16[2048,128]{1,0:T(8,128)(2,1)S(1)}, bf16[2048,128]{1,0:T(8,128)(2,1)}, u32[]{:S(2)}, u32[]{:S(2)}) collective-permute-start(bf16[2048,128]{1,0:T(8,128)(2,1)S(1)} %collective-permute-done.9.rest_1_), channel_id=1, source_target_pairs={{0,1},{1,0},{2,3},{3,2},{4,5},{5,4},{6,7},{7,6},{8,9},{9,8},{10,11... | collective-permute-start | bytes 1572872 | tf_op jit(solution)/shard_map/ppermute | solution.py:203
  43.2 6.9 %shard_map.59 = (bf16[2048,512]{1,0:T(8,128)(2,1)}, bf16[512,2048]{1,0:T(8,128)(2,1)}) custom-call(s32[6]{0:T(128)} %stack.54.places_ref, bf16[4,2,1024,128]{3,2,1,0:T(8,128)(2,1)} %bitcast.14.arrived_ref), custom_call_target="tpu_custom_call" | custom-call | bytes 6291456 | tf_op jit(solution)/shard_map/pallas_call | solution.py:27
  50.1 3.4 %collective-permute-done.11.rest_1_ = bf16[2048,128]{1,0:T(8,128)(2,1)S(1)} collective-permute-done((bf16[2048,128]{1,0:T(8,128)(2,1)}, bf16[2048,128]{1,0:T(8,128)(2,1)S(1)}, u32[]{:S(2)}, u32[]{:S(2)}) %collective-permute-start.11) | collective-permute-done | bytes 524320 | tf_op jit(solution)/shard_map/ppermute | solution.py:203
  53.6 3.3 %collective-permute-start.12 = (bf16[2048,128]{1,0:T(8,128)(2,1)S(1)}, bf16[2048,128]{1,0:T(8,128)(2,1)S(1)}, u32[]{:S(2)}, u32[]{:S(2)}) collective-permute-start(bf16[2048,128]{1,0:T(8,128)(2,1)S(1)} %collective-permute-done.11.rest_1_), channel_id=1, source_target_pairs={{0,1},{1,0},{2,3},{3,2},{4,5},{5,4},{6,7},{7,6},{8,9},{9,8},{10,11... | collective-permute-start | bytes 1572872 | tf_op jit(solution)/shard_map/ppermute | solution.py:203
  57.0 8.7 %shard_map.60.total_ref = f32[2048,128]{1,0:T(8,128)S(1)} custom-call(bf16[2048,8192]{1,0:T(8,128)(2,1)} %grad_ref.17, bf16[2048,512]{1,0:T(8,128)(2,1)} %get-tuple-element.34.prev_ref, f32[2048,1]{1,0:T(8,128)S(1)} %copy.9.bias_ref, f32[2048,128]{1,0:T(8,128)S(1)} %broadcast_in_dim.7.total_ref, bf16[8192,128]{1,0:T(8,128)(2,1)} %rest_0_.17, ...), custom_call_target="tpu_custom_call" | custom-call | flops 4294967296 | bytes 8388608 | tf_op jit(solution)/shard_map/pallas_call | solution.py:129
  65.7 9.2 %shard_map.61.total_ref = f32[2048,128]{1,0:T(8,128)S(1)} custom-call(bf16[2048,8192]{1,0:T(8,128)(2,1)} %grad_ref.17, bf16[2048,512]{1,0:T(8,128)(2,1)} %get-tuple-element.34.prev_ref, f32[2048,1]{1,0:T(8,128)S(1)} %copy.9.bias_ref, f32[2048,128]{1,0:T(8,128)S(1)} %shard_map.60.total_ref, bf16[8192,128]{1,0:T(8,128)(2,1)} %rest_0_.17, ...), custom_call_target="tpu_custom_call" | custom-call | flops 4294967296 | bytes 8388608 | tf_op jit(solution)/shard_map/pallas_call | solution.py:129
  74.9 8.7 %shard_map.62.total_ref = f32[2048,128]{1,0:T(8,128)S(1)} custom-call(bf16[2048,8192]{1,0:T(8,128)(2,1)} %grad_ref.17, bf16[2048,512]{1,0:T(8,128)(2,1)} %get-tuple-element.34.prev_ref, f32[2048,1]{1,0:T(8,128)S(1)} %copy.9.bias_ref, f32[2048,128]{1,0:T(8,128)S(1)} %shard_map.61.total_ref, bf16[8192,128]{1,0:T(8,128)(2,1)} %rest_0_.17, ...), custom_call_target="tpu_custom_call" | custom-call | flops 4294967296 | bytes 8388608 | tf_op jit(solution)/shard_map/pallas_call | solution.py:129
  83.7 8.7 %shard_map.63 = f32[2048,128]{1,0:T(8,128)S(1)} custom-call(bf16[2048,8192]{1,0:T(8,128)(2,1)} %grad_ref.17, bf16[2048,512]{1,0:T(8,128)(2,1)} %get-tuple-element.34.prev_ref, f32[2048,1]{1,0:T(8,128)S(1)} %copy.9.bias_ref, f32[2048,128]{1,0:T(8,128)S(1)} %shard_map.62.total_ref, bf16[8192,128]{1,0:T(8,128)(2,1)} %rest_0_.17, ...), custom_call_target="tpu_custom_call" | custom-call | flops 4294967296 | bytes 8388608 | tf_op jit(solution)/shard_map/pallas_call | solution.py:129
  92.7 1.6 collective-permute-start.17
  95.2 1.5 collective-permute-start.15
  99.5 2.5 broadcast_in_dim.8.total_ref
  102.0 23.8 %shard_map.64 = (f32[2048,512]{1,0:T(8,128)}, f32[2048,128]{1,0:T(8,128)}, f32[2048,128]{1,0:T(8,128)}, bf16[2048,256]{1,0:T(8,128)(2,1)}) custom-call(bf16[2048,8192]{1,0:T(8,128)(2,1)} %grad_ref.17, bf16[2048,512]{1,0:T(8,128)(2,1)} %get-tuple-element.34.prev_ref, bf16[512,2048]{1,0:T(8,128)(2,1)} %get-tuple-element.35.prev_t_ref, ...), custom_call_target="tpu_custom_call" | custom-call | flops 12884901888 | bytes 8388608 | tf_op jit(solution)/shard_map/pallas_call | solution.py:161
  125.9 1.4 collective-permute-start.18
  127.3 25.2 %shard_map.65 = (f32[2048,512]{1,0:T(8,128)}, f32[2048,128]{1,0:T(8,128)}, f32[2048,128]{1,0:T(8,128)}, bf16[2048,256]{1,0:T(8,128)(2,1)}) custom-call(bf16[2048,8192]{1,0:T(8,128)(2,1)} %grad_ref.17, bf16[2048,512]{1,0:T(8,128)(2,1)} %get-tuple-element.34.prev_ref, bf16[512,2048]{1,0:T(8,128)(2,1)} %get-tuple-element.35.prev_t_ref, ...), custom_call_target="tpu_custom_call" | custom-call | flops 12884901888 | bytes 8388608 | tf_op jit(solution)/shard_map/pallas_call | solution.py:161
  156.8 25.0 %shard_map.66 = (f32[2048,512]{1,0:T(8,128)}, f32[2048,128]{1,0:T(8,128)}, f32[2048,128]{1,0:T(8,128)}, bf16[2048,256]{1,0:T(8,128)(2,1)}) custom-call(bf16[2048,8192]{1,0:T(8,128)(2,1)} %grad_ref.17, bf16[2048,512]{1,0:T(8,128)(2,1)} %get-tuple-element.34.prev_ref, bf16[512,2048]{1,0:T(8,128)(2,1)} %get-tuple-element.35.prev_t_ref, ...), custom_call_target="tpu_custom_call" | custom-call | flops 12884901888 | bytes 8388608 | tf_op jit(solution)/shard_map/pallas_call | solution.py:161
  183.5 14.4 %shard_map.67 = (f32[1024,512]{1,0:T(8,128)}, f32[2048,512]{1,0:T(8,128)}) custom-call(bf16[2048,8192]{1,0:T(8,128)(2,1)} %grad_ref.17, bf16[2048,512]{1,0:T(8,128)(2,1)} %get-tuple-element.34.prev_ref, bf16[512,2048]{1,0:T(8,128)(2,1)} %get-tuple-element.35.prev_t_ref, f32[2048,1]{1,0:T(8,128)} %copy.16.bias_ref, f32[2048,1]{1,0:T(8,128)} %copy.17.dot_ref, ...), custom_call_target="tpu_custom_call" | custom-call | flops 6442450944 | bytes 4194304 | tf_op jit(solution)/shard_map/pallas_call | solution.py:161
  197.9 2.3 dynamic-slice_convert_fusion.3
  200.2 1.6 collective-permute-start.21
  201.8 2.5 collective-permute-start.22
  204.3 14.4 %shard_map.68 = (f32[1024,512]{1,0:T(8,128)}, f32[2048,128]{1,0:T(8,128)}, f32[2048,128]{1,0:T(8,128)}, bf16[2048,256]{1,0:T(8,128)(2,1)}) custom-call(bf16[2048,8192]{1,0:T(8,128)(2,1)} %grad_ref.17, bf16[2048,512]{1,0:T(8,128)(2,1)} %get-tuple-element.34.prev_ref, bf16[512,2048]{1,0:T(8,128)(2,1)} %get-tuple-element.35.prev_t_ref, ...), custom_call_target="tpu_custom_call" | custom-call | flops 6442450944 | bytes 4194304 | tf_op jit(solution)/shard_map/pallas_call | solution.py:161
  221.5 3.1 %collective-permute-done.22 = bf16[1024,128]{1,0:T(8,128)(2,1)} collective-permute-done((bf16[1024,128]{1,0:T(8,128)(2,1)}, bf16[1024,128]{1,0:T(8,128)(2,1)}, u32[]{:S(2)}, u32[]{:S(2)}) %collective-permute-start.22) | collective-permute-done | bytes 262176 | tf_op jit(solution)/shard_map/ppermute | solution.py:206
  224.6 2.4 collective-permute-done.23
  231.2 2.9 %collective-permute-done.30 = bf16[2048,128]{1,0:T(8,128)(2,1)S(1)} collective-permute-done((bf16[2048,128]{1,0:T(8,128)(2,1)S(1)}, bf16[2048,128]{1,0:T(8,128)(2,1)S(1)}, u32[]{:S(2)}, u32[]{:S(2)}) %collective-permute-start.30) | collective-permute-done | bytes 524320 | tf_op jit(solution)/shard_map/ppermute | solution.py:203
  235.5 15.0 %collective-permute-done.26 = bf16[1024,128]{1,0:T(8,128)(2,1)S(1)} collective-permute-done((bf16[1024,128]{1,0:T(8,128)(2,1)S(1)}, bf16[1024,128]{1,0:T(8,128)(2,1)S(1)}, u32[]{:S(2)}, u32[]{:S(2)}) %collective-permute-start.26) | collective-permute-done | bytes 262176 | tf_op jit(solution)/shard_map/ppermute | solution.py:206
  250.5 2.4 collective-permute-done.27
  254.2 2.3 pad_maximum_fusion
  (106 shorter events, 36.4 us)
Async XLA Ops:
  2.5 22.3 %collective-permute-start.2 = (bf16[1024,128]{1,0:T(8,128)(2,1)}, bf16[1024,128]{1,0:T(8,128)(2,1)S(1)}, u32[]{:S(2)}, u32[]{:S(2)}) collective-permute-start(bf16[1024,128]{1,0:T(8,128)(2,1)} %get-tuple-element.67), channel_id=1, source_target_pairs={{0,8},{4,12},{8,0},{12,4},{1,9},{5,13},{9,1},{13,5},{2,10},{6,14},... | collective-permute-start | bytes 786440 | tf_op jit(solution)/shard_map/ppermute | solution.py:206
  4.8 16.5 %collective-permute-start = (bf16[1024,128]{1,0:T(8,128)(2,1)}, bf16[1024,128]{1,0:T(8,128)(2,1)S(1)}, u32[]{:S(2)}, u32[]{:S(2)}) collective-permute-start(bf16[1024,128]{1,0:T(8,128)(2,1)} %get-tuple-element.67), channel_id=1, source_target_pairs={{0,12},{4,0},{8,4},{12,8},{1,13},{5,1},{9,5},{13,9},{2,14},{6,2},{... | collective-permute-start | bytes 786440 | tf_op jit(solution)/shard_map/ppermute | solution.py:206
  4.9 51.9 %collective-permute-start.7 = (bf16[8192,128]{1,0:T(8,128)(2,1)}, bf16[8192,128]{1,0:T(8,128)(2,1)}, u32[]{:S(2)}, u32[]{:S(2)}) collective-permute-start(bf16[8192,128]{1,0:T(8,128)(2,1)} %rest_0_.17), channel_id=1, source_target_pairs={{0,1},{1,0},{2,3},{3,2},{4,5},{5,4},{6,7},{7,6},{8,9},{9,8},{10,11... | collective-permute-start | bytes 6291464 | tf_op jit(solution)/shard_map/ppermute | solution.py:203
  8.8 23.5 %collective-permute-start.9 = (bf16[2048,128]{1,0:T(8,128)(2,1)S(1)}, bf16[2048,128]{1,0:T(8,128)(2,1)S(1)}, u32[]{:S(2)}, u32[]{:S(2)}) collective-permute-start(bf16[2048,128]{1,0:T(8,128)(2,1)S(1)} %get-tuple-element.76), channel_id=1, source_target_pairs={{0,2},{1,3},{2,0},{3,1},{4,6},{5,7},{6,4},{7,5},{8,10},{9,11},{10,... | collective-permute-start | bytes 1572872 | tf_op jit(solution)/shard_map/ppermute | solution.py:203
  10.0 23.7 %collective-permute-start.6 = (bf16[2048,128]{1,0:T(8,128)(2,1)}, bf16[2048,128]{1,0:T(8,128)(2,1)}, u32[]{:S(2)}, u32[]{:S(2)}) collective-permute-start(bf16[2048,128]{1,0:T(8,128)(2,1)} %get-tuple-element.77), channel_id=1, source_target_pairs={{0,2},{1,3},{2,0},{3,1},{4,6},{5,7},{6,4},{7,5},{8,10},{9,11},{10,... | collective-permute-start | bytes 1572872 | tf_op jit(solution)/shard_map/ppermute | solution.py:203
  21.3 6.7 %collective-permute-start.1 = (bf16[1024,128]{1,0:T(8,128)(2,1)S(1)}, bf16[1024,128]{1,0:T(8,128)(2,1)S(1)}, u32[]{:S(2)}, u32[]{:S(2)}) collective-permute-start(bf16[1024,128]{1,0:T(8,128)(2,1)S(1)} %collective-permute-done), channel_id=1, source_target_pairs={{0,16},{16,0},{1,17},{17,1},{2,18},{18,2},{3,19},{19,3},{4,20},{20... | collective-permute-start | bytes 786440 | tf_op jit(solution)/shard_map/ppermute | solution.py:209
  24.8 6.3 %collective-permute-start.4 = (bf16[1024,128]{1,0:T(8,128)(2,1)}, bf16[1024,128]{1,0:T(8,128)(2,1)S(1)}, u32[]{:S(2)}, u32[]{:S(2)}) collective-permute-start(bf16[1024,128]{1,0:T(8,128)(2,1)} %get-tuple-element.67), channel_id=1, source_target_pairs={{0,4},{4,8},{8,12},{12,0},{1,5},{5,9},{9,13},{13,1},{2,6},{6,10},{... | collective-permute-start | bytes 786440 | tf_op jit(solution)/shard_map/ppermute | solution.py:206
  27.9 7.0 %collective-permute-start.3 = (bf16[1024,128]{1,0:T(8,128)(2,1)S(1)}, bf16[1024,128]{1,0:T(8,128)(2,1)S(1)}, u32[]{:S(2)}, u32[]{:S(2)}) collective-permute-start(bf16[1024,128]{1,0:T(8,128)(2,1)S(1)} %collective-permute-done.2), channel_id=1, source_target_pairs={{0,16},{16,0},{1,17},{17,1},{2,18},{18,2},{3,19},{19,3},{4,20},{20... | collective-permute-start | bytes 786440 | tf_op jit(solution)/shard_map/ppermute | solution.py:209
  31.1 19.0 %collective-permute-start.13 = (bf16[2048,128]{1,0:T(8,128)(2,1)S(1)}, bf16[2048,128]{1,0:T(8,128)(2,1)S(1)}, u32[]{:S(2)}, u32[]{:S(2)}) collective-permute-start(bf16[2048,128]{1,0:T(8,128)(2,1)S(1)} %get-tuple-element.74), channel_id=1, source_target_pairs={{0,2},{1,3},{2,0},{3,1},{4,6},{5,7},{6,4},{7,5},{8,10},{9,11},{10,... | collective-permute-start | bytes 1572872 | tf_op jit(solution)/shard_map/ppermute | solution.py:203
  32.3 21.3 %collective-permute-start.11 = (bf16[2048,128]{1,0:T(8,128)(2,1)}, bf16[2048,128]{1,0:T(8,128)(2,1)S(1)}, u32[]{:S(2)}, u32[]{:S(2)}) collective-permute-start(bf16[2048,128]{1,0:T(8,128)(2,1)} %get-tuple-element.75), channel_id=1, source_target_pairs={{0,2},{1,3},{2,0},{3,1},{4,6},{5,7},{6,4},{7,5},{8,10},{9,11},{10,... | collective-permute-start | bytes 1572872 | tf_op jit(solution)/shard_map/ppermute | solution.py:203
  33.7 5.8 %collective-permute-start.5 = (bf16[1024,128]{1,0:T(8,128)(2,1)S(1)}, bf16[1024,128]{1,0:T(8,128)(2,1)S(1)}, u32[]{:S(2)}, u32[]{:S(2)}) collective-permute-start(bf16[1024,128]{1,0:T(8,128)(2,1)S(1)} %collective-permute-done.4), channel_id=1, source_target_pairs={{0,16},{16,0},{1,17},{17,1},{2,18},{18,2},{3,19},{19,3},{4,20},{20... | collective-permute-start | bytes 786440 | tf_op jit(solution)/shard_map/ppermute | solution.py:209
  35.0 21.9 %collective-permute-start.8 = (bf16[2048,128]{1,0:T(8,128)(2,1)}, bf16[2048,128]{1,0:T(8,128)(2,1)}, u32[]{:S(2)}, u32[]{:S(2)}) collective-permute-start(bf16[2048,128]{1,0:T(8,128)(2,1)} %collective-permute-done.6.rest_1_), channel_id=1, source_target_pairs={{0,1},{1,0},{2,3},{3,2},{4,5},{5,4},{6,7},{7,6},{8,9},{9,8},{10,11... | collective-permute-start | bytes 1572872 | tf_op jit(solution)/shard_map/ppermute | solution.py:203
  39.5 26.2 %collective-permute-start.10 = (bf16[2048,128]{1,0:T(8,128)(2,1)S(1)}, bf16[2048,128]{1,0:T(8,128)(2,1)}, u32[]{:S(2)}, u32[]{:S(2)}) collective-permute-start(bf16[2048,128]{1,0:T(8,128)(2,1)S(1)} %collective-permute-done.9.rest_1_), channel_id=1, source_target_pairs={{0,1},{1,0},{2,3},{3,2},{4,5},{5,4},{6,7},{7,6},{8,9},{9,8},{10,11... | collective-permute-start | bytes 1572872 | tf_op jit(solution)/shard_map/ppermute | solution.py:203
  50.1 33.6 %collective-permute-start.14 = (bf16[2048,128]{1,0:T(8,128)(2,1)S(1)}, bf16[2048,128]{1,0:T(8,128)(2,1)S(1)}, u32[]{:S(2)}, u32[]{:S(2)}) collective-permute-start(bf16[2048,128]{1,0:T(8,128)(2,1)S(1)} %collective-permute-done.13.rest_1_), channel_id=1, source_target_pairs={{0,1},{1,0},{2,3},{3,2},{4,5},{5,4},{6,7},{7,6},{8,9},{9,8},{10,11... | collective-permute-start | bytes 1572872 | tf_op jit(solution)/shard_map/ppermute | solution.py:203
  53.6 21.4 %collective-permute-start.12 = (bf16[2048,128]{1,0:T(8,128)(2,1)S(1)}, bf16[2048,128]{1,0:T(8,128)(2,1)S(1)}, u32[]{:S(2)}, u32[]{:S(2)}) collective-permute-start(bf16[2048,128]{1,0:T(8,128)(2,1)S(1)} %collective-permute-done.11.rest_1_), channel_id=1, source_target_pairs={{0,1},{1,0},{2,3},{3,2},{4,5},{5,4},{6,7},{7,6},{8,9},{9,8},{10,11... | collective-permute-start | bytes 1572872 | tf_op jit(solution)/shard_map/ppermute | solution.py:203
  92.7 5.4 %collective-permute-start.17 = (f32[16,128]{1,0:T(8,128)S(1)}, f32[16,128]{1,0:T(8,128)S(1)}, u32[]{:S(2)}, u32[]{:S(2)}) collective-permute-start(f32[16,128]{1,0:T(8,128)S(1)} %bitcast.30), channel_id=1, source_target_pairs={{0,12},{4,0},{8,4},{12,8},{1,13},{5,1},{9,5},{13,9},{2,14},{6,2},{... | collective-permute-start | bytes 24584 | tf_op jit(solution)/shard_map/ppermute | solution.py:206
  94.3 3.8 %collective-permute-start.16 = (f32[16,128]{1,0:T(8,128)S(1)}, f32[16,128]{1,0:T(8,128)S(1)}, u32[]{:S(2)}, u32[]{:S(2)}) collective-permute-start(f32[16,128]{1,0:T(8,128)S(1)} %bitcast.31), channel_id=1, source_target_pairs={{0,8},{4,12},{8,0},{12,4},{1,9},{5,13},{9,1},{13,5},{2,10},{6,14},... | collective-permute-start | bytes 24584 | tf_op jit(solution)/shard_map/ppermute | solution.py:206
  95.2 2.9 %collective-permute-start.15 = (f32[16,128]{1,0:T(8,128)S(1)}, f32[16,128]{1,0:T(8,128)S(1)}, u32[]{:S(2)}, u32[]{:S(2)}) collective-permute-start(f32[16,128]{1,0:T(8,128)S(1)} %bitcast.32), channel_id=1, source_target_pairs={{0,4},{4,8},{8,12},{12,0},{1,5},{5,9},{9,13},{13,1},{2,6},{6,10},{... | collective-permute-start | bytes 24584 | tf_op jit(solution)/shard_map/ppermute | solution.py:206
  125.9 26.8 %collective-permute-start.18 = (bf16[2048,256]{1,0:T(8,128)(2,1)}, bf16[2048,256]{1,0:T(8,128)(2,1)}, u32[]{:S(2)}, u32[]{:S(2)}) collective-permute-start(bf16[2048,256]{1,0:T(8,128)(2,1)} %get-tuple-element.39), channel_id=1, source_target_pairs={{0,1},{1,0},{2,3},{3,2},{4,5},{5,4},{6,7},{7,6},{8,9},{9,8},{10,11... | collective-permute-start | bytes 3145736 | tf_op jit(solution)/shard_map/ppermute | solution.py:203
  152.5 2.9 %collective-permute-start.19 = (bf16[2048,256]{1,0:T(8,128)(2,1)}, bf16[2048,256]{1,0:T(8,128)(2,1)S(1)}, u32[]{:S(2)}, u32[]{:S(2)}) collective-permute-start(bf16[2048,256]{1,0:T(8,128)(2,1)} %get-tuple-element.43), channel_id=1, source_target_pairs={{0,1},{1,0},{2,3},{3,2},{4,5},{5,4},{6,7},{7,6},{8,9},{9,8},{10,11... | collective-permute-start | bytes 3145736 | tf_op jit(solution)/shard_map/ppermute | solution.py:203
  153.9 28.4 %collective-permute-start.20 = (bf16[2048,128]{1,0:T(8,128)(2,1)S(1)}, bf16[2048,128]{1,0:T(8,128)(2,1)S(1)}, u32[]{:S(2)}, u32[]{:S(2)}) collective-permute-start(bf16[2048,128]{1,0:T(8,128)(2,1)S(1)} %add_convert_fusion.3), channel_id=1, source_target_pairs={{0,2},{1,3},{2,0},{3,1},{4,6},{5,7},{6,4},{7,5},{8,10},{9,11},{10,... | collective-permute-start | bytes 1572872 | tf_op jit(solution)/shard_map/ppermute | solution.py:203
  155.6 63.2 %collective-permute-start.28 = (bf16[2048,128]{1,0:T(8,128)(2,1)S(1)}, bf16[2048,128]{1,0:T(8,128)(2,1)S(1)}, u32[]{:S(2)}, u32[]{:S(2)}) collective-permute-start(bf16[2048,128]{1,0:T(8,128)(2,1)S(1)} %add_convert_fusion.2), channel_id=1, source_target_pairs={{0,2},{1,3},{2,0},{3,1},{4,6},{5,7},{6,4},{7,5},{8,10},{9,11},{10,... | collective-permute-start | bytes 1572872 | tf_op jit(solution)/shard_map/ppermute | solution.py:203
  181.9 38.7 %collective-permute-start.29 = (bf16[2048,256]{1,0:T(8,128)(2,1)}, bf16[2048,256]{1,0:T(8,128)(2,1)S(1)}, u32[]{:S(2)}, u32[]{:S(2)}) collective-permute-start(bf16[2048,256]{1,0:T(8,128)(2,1)} %get-tuple-element.62), channel_id=1, source_target_pairs={{0,1},{1,0},{2,3},{3,2},{4,5},{5,4},{6,7},{7,6},{8,9},{9,8},{10,11... | collective-permute-start | bytes 3145736 | tf_op jit(solution)/shard_map/ppermute | solution.py:203
  200.2 21.3 %collective-permute-start.21 = (bf16[1024,128]{1,0:T(8,128)(2,1)}, bf16[1024,128]{1,0:T(8,128)(2,1)}, u32[]{:S(2)}, u32[]{:S(2)}) collective-permute-start(bf16[1024,128]{1,0:T(8,128)(2,1)} %get-tuple-element.48), channel_id=1, source_target_pairs={{0,4},{4,8},{8,12},{12,0},{1,5},{5,9},{9,13},{13,1},{2,6},{6,10},{... | collective-permute-start | bytes 786440 | tf_op jit(solution)/shard_map/ppermute | solution.py:206
  201.8 22.8 %collective-permute-start.22 = (bf16[1024,128]{1,0:T(8,128)(2,1)}, bf16[1024,128]{1,0:T(8,128)(2,1)}, u32[]{:S(2)}, u32[]{:S(2)}) collective-permute-start(bf16[1024,128]{1,0:T(8,128)(2,1)} %get-tuple-element.49), channel_id=1, source_target_pairs={{0,8},{4,12},{8,0},{12,4},{1,9},{5,13},{9,1},{13,5},{2,10},{6,14},... | collective-permute-start | bytes 786440 | tf_op jit(solution)/shard_map/ppermute | solution.py:206
  204.3 22.7 %collective-permute-start.23 = (bf16[1024,128]{1,0:T(8,128)(2,1)S(1)}, bf16[1024,128]{1,0:T(8,128)(2,1)}, u32[]{:S(2)}, u32[]{:S(2)}) collective-permute-start(bf16[1024,128]{1,0:T(8,128)(2,1)S(1)} %get-tuple-element.50), channel_id=1, source_target_pairs={{0,12},{4,0},{8,4},{12,8},{1,13},{5,1},{9,5},{13,9},{2,14},{6,2},{... | collective-permute-start | bytes 786440 | tf_op jit(solution)/shard_map/ppermute | solution.py:206
  218.7 9.7 %collective-permute-start.24 = (bf16[2048,256]{1,0:T(8,128)(2,1)}, bf16[2048,256]{1,0:T(8,128)(2,1)S(1)}, u32[]{:S(2)}, u32[]{:S(2)}) collective-permute-start(bf16[2048,256]{1,0:T(8,128)(2,1)} %get-tuple-element.55), channel_id=1, source_target_pairs={{0,1},{1,0},{2,3},{3,2},{4,5},{5,4},{6,7},{7,6},{8,9},{9,8},{10,11... | collective-permute-start | bytes 3145736 | tf_op jit(solution)/shard_map/ppermute | solution.py:203
  221.0 13.2 %collective-permute-start.30 = (bf16[2048,128]{1,0:T(8,128)(2,1)S(1)}, bf16[2048,128]{1,0:T(8,128)(2,1)S(1)}, u32[]{:S(2)}, u32[]{:S(2)}) collective-permute-start(bf16[2048,128]{1,0:T(8,128)(2,1)S(1)} %add_convert_fusion), channel_id=1, source_target_pairs={{0,2},{1,3},{2,0},{3,1},{4,6},{5,7},{6,4},{7,5},{8,10},{9,11},{10,... | collective-permute-start | bytes 1572872 | tf_op jit(solution)/shard_map/ppermute | solution.py:203
  228.5 7.0 %collective-permute-start.25 = (bf16[1024,128]{1,0:T(8,128)(2,1)S(1)}, bf16[1024,128]{1,0:T(8,128)(2,1)S(1)}, u32[]{:S(2)}, u32[]{:S(2)}) collective-permute-start(bf16[1024,128]{1,0:T(8,128)(2,1)S(1)} %get-tuple-element.56), channel_id=1, source_target_pairs={{0,4},{4,8},{8,12},{12,0},{1,5},{5,9},{9,13},{13,1},{2,6},{6,10},{... | collective-permute-start | bytes 786440 | tf_op jit(solution)/shard_map/ppermute | solution.py:206
  228.6 21.9 %collective-permute-start.26 = (bf16[1024,128]{1,0:T(8,128)(2,1)S(1)}, bf16[1024,128]{1,0:T(8,128)(2,1)S(1)}, u32[]{:S(2)}, u32[]{:S(2)}) collective-permute-start(bf16[1024,128]{1,0:T(8,128)(2,1)S(1)} %get-tuple-element.57), channel_id=1, source_target_pairs={{0,8},{4,12},{8,0},{12,4},{1,9},{5,13},{9,1},{13,5},{2,10},{6,14},... | collective-permute-start | bytes 786440 | tf_op jit(solution)/shard_map/ppermute | solution.py:206
  229.4 23.6 %collective-permute-start.27 = (bf16[1024,128]{1,0:T(8,128)(2,1)S(1)}, bf16[1024,128]{1,0:T(8,128)(2,1)S(1)}, u32[]{:S(2)}, u32[]{:S(2)}) collective-permute-start(bf16[1024,128]{1,0:T(8,128)(2,1)S(1)} %get-tuple-element.58), channel_id=1, source_target_pairs={{0,12},{4,0},{8,4},{12,8},{1,13},{5,1},{9,5},{13,9},{2,14},{6,2},{... | collective-permute-start | bytes 786440 | tf_op jit(solution)/shard_map/ppermute | solution.py:206
  230.7 23.3 %collective-permute-start.31 = (bf16[2048,128]{1,0:T(8,128)(2,1)S(1)}, bf16[2048,128]{1,0:T(8,128)(2,1)S(1)}, u32[]{:S(2)}, u32[]{:S(2)}) collective-permute-start(bf16[2048,128]{1,0:T(8,128)(2,1)S(1)} %add_convert_fusion.1), channel_id=1, source_target_pairs={{0,2},{1,3},{2,0},{3,1},{4,6},{5,7},{6,4},{7,5},{8,10},{9,11},{10,... | collective-permute-start | bytes 1572872 | tf_op jit(solution)/shard_map/ppermute | solution.py:203
  (16 other events, 247.5 us)
